TPU v7x, 256 devices: a whole 4x4x8 slice. The times are simulated.
256 devices in a mesh: serve: 128 (over y, x, z), rep: 2 (over core).
Axes of the slice: x: 4, y: 4, z: 8, core: 2. Of those that a mesh axis runs over, the one named last changes fastest.
Arguments:
- history: bfloat16 [131072, 1024], P(('serve', 'rep')), may hold values from -6 to 6
- candidates: bfloat16 [65536, 1024], P(('serve', 'rep')), may hold values from -6 to 6
- cand_user: int32 [65536, 1], P(('serve', 'rep')), may hold values from 0 to 127; in each aligned block of 256 rows (0 to 255, 256 to 511, ...) at most 4 rows name the same one
- hist_len: int32 [128], P('serve'), may hold values from 1 to 1024, as said below
- w_uvqk: bfloat16 [1024, 4096], replicated, may hold values from -0.1875 to 0.1875
- w_out: bfloat16 [1024, 1024], replicated, may hold values from -0.1875 to 0.1875
Outputs:
- scored: bfloat16 [65536, 1024], P(('serve', 'rep'))
Inputs may be any that keep to these rules, and one draw needn't show every extreme that they name: `cand_user`: in each aligned block of 256 rows no user is named more than 4 times, a bound that some block reaches. `hist_len`: some user has exactly 1024 valid events.
All inputs are finite; a program needn't handle non-finite values.
Results may differ from a plain program's by a relative error of at most 0.007.
Values may be sent and summed in bfloat16 or wider, within the bound.
No kernel may reach another device: no remote copies, remote signals or barrier semaphores. Data moves between devices by JAX's collectives and lax.ppermute only.
A program may use at most 64 MiB of HBM per device.

v0:
```python
import math

import jax
import jax.numpy as jnp
from jax import lax
from jax.sharding import PartitionSpec as P

HEADS = 8


def silu_rows(matrix, weight):
    return jax.nn.silu(jnp.dot(matrix, weight, preferred_element_type=jnp.float32)).astype(
        jnp.bfloat16
    )


def history_attention(queries, keys_vals, length):
    feature_width = queries.shape[1]
    head_size = feature_width // HEADS
    key_rows = keys_vals[:, :feature_width].reshape(-1, HEADS, head_size)
    value_rows = keys_vals[:, feature_width:].reshape(-1, HEADS, head_size)
    query_rows = queries.reshape(-1, HEADS, head_size)
    scores = jnp.einsum(
        "ihd,jhd->hij", query_rows, key_rows, preferred_element_type=jnp.float32
    ) / math.sqrt(head_size)
    key_mask = (jnp.arange(key_rows.shape[0], dtype=jnp.int32) < length).astype(jnp.float32)
    weights = (jax.nn.silu(scores) * key_mask[None, None, :]).astype(jnp.bfloat16)
    result = jnp.einsum("hij,jhd->ihd", weights, value_rows, preferred_element_type=jnp.float32)
    return result.reshape(-1, feature_width).astype(jnp.bfloat16)


def finish(candidates, projected, history_part, w_out):
    feature_width = candidates.shape[1]
    head_size = feature_width // HEADS
    gate_rows = projected[:, :feature_width].astype(jnp.float32)
    value_rows = (
        projected[:, feature_width : 2 * feature_width]
        .reshape(-1, HEADS, head_size)
        .astype(jnp.float32)
    )
    query_rows = (
        projected[:, 2 * feature_width : 3 * feature_width]
        .reshape(-1, HEADS, head_size)
        .astype(jnp.float32)
    )
    key_rows = projected[:, 3 * feature_width :].reshape(-1, HEADS, head_size).astype(jnp.float32)
    self_scores = jnp.sum(query_rows * key_rows, -1) / math.sqrt(head_size)
    self_term = (jax.nn.silu(self_scores)[:, :, None] * value_rows).reshape(-1, feature_width)
    attended = history_part + self_term
    row_mean = jnp.mean(attended, 1, keepdims=True)
    row_var = jnp.mean(jnp.square(attended - row_mean), 1, keepdims=True)
    normed = ((attended - row_mean) * lax.rsqrt(row_var + 1e-05) * gate_rows).astype(jnp.bfloat16)
    output = candidates.astype(jnp.float32) + jnp.dot(
        normed, w_out, preferred_element_type=jnp.float32
    )
    return output.astype(jnp.bfloat16)


def per_device(history, candidates, cand_user, hist_len, w_uvqk, w_out):
    feature_width = candidates.shape[1]
    w_kv = jnp.concatenate(
        [w_uvqk[:, 3 * feature_width :], w_uvqk[:, feature_width : 2 * feature_width]], 1
    )
    keys_vals = lax.all_gather(silu_rows(history, w_kv), "rep", axis=0, tiled=True)
    projected = silu_rows(candidates, w_uvqk)
    query_self = projected[:, 2 * feature_width : 3 * feature_width]
    servers = lax.axis_size("serve")
    row_count = candidates.shape[0]
    capacity = max(2, 2 * row_count // servers)
    user_ids = cand_user[:, 0]
    one_hot = (user_ids[:, None] == jnp.arange(servers, dtype=jnp.int32)[None, :]).astype(jnp.int32)
    before = jnp.cumsum(one_hot, 0) - one_hot
    slot_rank = jnp.sum(before * one_hot, 1)
    slot_index = user_ids * capacity + slot_rank
    placement = (
        jnp.arange(servers * capacity, dtype=jnp.int32)[:, None] == slot_index[None, :]
    ).astype(jnp.bfloat16)
    outgoing = jnp.dot(placement, query_self, preferred_element_type=jnp.float32).astype(
        jnp.bfloat16
    )
    outgoing = outgoing.reshape(servers, capacity, feature_width)
    length = hist_len[0]
    received = lax.all_to_all(outgoing, "serve", split_axis=0, concat_axis=0, tiled=True)
    partial_rows = history_attention(received.reshape(-1, feature_width), keys_vals, length)
    partial_rows = partial_rows.reshape(received.shape)
    returned = lax.all_to_all(partial_rows, "serve", split_axis=0, concat_axis=0, tiled=True)
    history_part = jnp.dot(
        placement.T, returned.reshape(-1, feature_width), preferred_element_type=jnp.float32
    )
    return finish(candidates, projected, history_part, w_out)


def solution(mesh):
    placed = (
        P(("serve", "rep"), None),
        P(("serve", "rep"), None),
        P(("serve", "rep"), None),
        P("serve"),
        P(),
        P(),
    )
    return jax.shard_map(
        per_device, mesh=mesh, in_specs=placed, out_specs=P(("serve", "rep"), None), check_vma=False
    )
```

profile of v0, /device:TPU:32, one launch (start us, length us, event | category | flops | bytes accessed | tf_op | source)
XLA Modules:
  0.0 140.0 jit_solution(1243205983566059240)
XLA Ops:
  6.5 2.8 %fusion.31 = (bf16[1024,1024]{1,0:T(8,128)(2,1)S(1)}, bf16[1024,1024]{1,0:T(8,128)(2,1)S(1)}) fusion(bf16[1024,4096]{1,0:T(8,128)(2,1)} %param.10), kind=kLoop, calls=%fused_computation.50 | loop fusion | bytes 8388608 | tf_op jit(solution)/shard_map/slice | solution.py:62
  9.4 4.5 %fusion.7 = bf16[512,2048]{0,1:T(8,128)(2,1)} fusion(bf16[512,1024]{1,0:T(8,128)(2,1)S(1)} %copy-done.4, bf16[1024,1024]{1,0:T(8,128)(2,1)S(1)} %get-tuple-element.6, bf16[1024,1024]{1,0:T(8,128)(2,1)S(1)} %get-tuple-element.5), kind=kOutput, calls=%fused_computation.11 | convolution fusion | flops 2161115136 | bytes 7340032 | tf_op jit(solution)/shard_map/dot_general | solution.py:12
  14.0 0.2 fusion.22
  14.5 6.0 %multiply_convert_fusion.1 = bf16[256,4096]{1,0:T(8,128)(2,1)S(1)} fusion(bf16[256,1024]{1,0:T(8,128)(2,1)} %param.7, bf16[1024,4096]{1,0:T(8,128)(2,1)} %param.10), kind=kOutput, calls=%fused_computation.10 | convolution fusion | flops 2152726528 | bytes 11010048 | tf_op jit(solution)/shard_map/dot_general | solution.py:12
  20.6 1.3 copy-done.1
  21.9 0.4 convolution_convert_fusion
  22.4 1.3 reshape.75
  23.7 15.0 %all-to-all-start = ((bf16[128,4,1024]{2,1,0:T(4,128)(2,1)}), bf16[128,4,1024]{2,1,0:T(4,128)(2,1)S(1)}, u32[]{:S(2)}, u32[]{:S(2)}) async-start(bf16[128,4,1024]{2,1,0:T(4,128)(2,1)} %reshape.75), calls=%async_computation | async-start | bytes 2097152 | tf_op jit(solution)/shard_map/all_to_all | solution.py:83
  39.3 30.7 %all-to-all-done = bf16[128,4,1024]{2,1,0:T(4,128)(2,1)S(1)} async-done(((bf16[128,4,1024]{2,1,0:T(4,128)(2,1)}), bf16[128,4,1024]{2,1,0:T(4,128)(2,1)S(1)}, u32[]{:S(2)}, u32[]{:S(2)}) %all-to-all-start) | async-done | bytes 1048608 | tf_op jit(solution)/shard_map/all_to_all | solution.py:83
  70.0 1.2 reshape_reshape.3
  71.2 4.8 %fusion.32 = (bf16[1024,1024]{0,1:T(8,128)(2,1)}, bf16[1024,1024]{0,1:T(8,128)(2,1)}) fusion(bf16[1024,2048]{0,1:T(8,128)(2,1)} %all-gather.2.cloned.1.call-done), kind=kLoop, calls=%fused_computation.51 | loop fusion | bytes 8388608 | tf_op jit(solution)/shard_map/slice | solution.py:20
  76.0 10.7 %fusion.12 = bf16[512,8,128]{0,2,1:T(8,128)(2,1)} fusion(bf16[1024,8,128]{0,2,1:T(8,128)(2,1)} %bitcast.52, bf16[1024,8,128]{0,2,1:T(8,128)(2,1)} %bitcast.51, f32[1024]{0:T(1024)S(1)} %fusion.27, bf16[512,8,128]{2,1,0:T(8,128)(2,1)S(1)} %copy-done.2), kind=kOutput, calls=%fused_computation.15 | convolution fusion | flops 2177368064 | bytes 6295552 | tf_op jit(solution)/shard_map/hij,jhd->ihd/dot_general | solution.py:28
  86.8 1.7 %copy.24 = bf16[512,8,128]{2,1,0:T(8,128)(2,1)S(1)} copy(bf16[512,8,128]{0,2,1:T(8,128)(2,1)} %fusion.12) | data formatting | bytes 2097152 | tf_op jit(solution)/shard_map/convert_element_type | solution.py:29
  88.5 1.2 convert_element_type.71
  89.7 7.7 %all-to-all-start.1 = ((bf16[128,4,1024]{2,1,0:T(4,128)(2,1)}), bf16[128,4,1024]{2,1,0:T(4,128)(2,1)}, u32[]{:S(2)}, u32[]{:S(2)}) async-start(bf16[128,4,1024]{2,1,0:T(4,128)(2,1)} %convert_element_type.71), calls=%async_computation.1 | async-start | bytes 2097152 | tf_op jit(solution)/shard_map/all_to_all | solution.py:86
  97.4 1.4 multiply_bitcast_fusion
  98.7 0.2 copy.28
  98.9 0.3 reduce_sum.37
  99.5 27.3 %all-to-all-done.1 = bf16[128,4,1024]{2,1,0:T(4,128)(2,1)} async-done(((bf16[128,4,1024]{2,1,0:T(4,128)(2,1)}), bf16[128,4,1024]{2,1,0:T(4,128)(2,1)}, u32[]{:S(2)}, u32[]{:S(2)}) %all-to-all-start.1) | async-done | bytes 1048608 | tf_op jit(solution)/shard_map/all_to_all | solution.py:86
  126.8 1.3 reshape.77
  128.2 0.3 mul.80
  128.5 1.7 %fusion.33 = (f32[256]{0:T(256)S(1)}, f32[256,1024]{1,0:T(8,128)S(1)}) fusion(bf16[256,4096]{1,0:T(8,128)(2,1)} %copy-done.1, f32[32,8,8,128]{3,2,1,0:T(8,128)S(1)} %bitcast.49, bf16[512,1024]{1,0:T(8,128)(2,1)S(1)} %reshape.77, s32[256]{0:T(256)S(1)} %multiply_add_fusion), kind=kOutput, calls=%fused_computation.52 | convolution fusion | flops 269614848 | bytes 3672064 | tf_op jit(solution)/shard_map/dot_general | solution.py:87
  130.2 0.3 multiply_reduce_fusion
  130.5 2.6 %fusion.13 = bf16[256,1024]{1,0:T(8,128)(2,1)} fusion(bf16[1024,1024]{1,0:T(8,128)(2,1)S(1)} %copy-done, bf16[256,1024]{1,0:T(8,128)(2,1)S(1)} %copy-done.5, f32[256,1024]{1,0:T(8,128)S(1)} %get-tuple-element.10, bf16[256,4096]{1,0:T(8,128)(2,1)} %copy-done.1, f32[256]{0:T(256)S(1)} %add_rsqrt_fusion, f32[256]{0:T(256)S(1)} %broadcast_multiply_fusion), kind=kOutput, calls=%fused_computation.18 | convolution fusion | flops 538968064 | bytes 4720640 | tf_op jit(solution)/shard_map/dot_general | solution.py:53
  (29 shorter events, 0.6 us)
Async XLA Ops:
  6.5 123.9 %copy-start = (bf16[1024,1024]{1,0:T(8,128)(2,1)S(1)}, bf16[1024,1024]{1,0:T(8,128)(2,1)}, u32[]{:S(2)}) copy-start(bf16[1024,1024]{1,0:T(8,128)(2,1)} %param.11) | copy-start | bytes 6291460
  6.5 2.8 %copy-start.4 = (bf16[512,1024]{1,0:T(8,128)(2,1)S(1)}, bf16[512,1024]{1,0:T(8,128)(2,1)}, u32[]{:S(2)}) copy-start(bf16[512,1024]{1,0:T(8,128)(2,1)} %param.6) | copy-start | bytes 3145732
  6.5 64.7 %all-gather.2.cloned.1.call-start = ((), (), s32[]{:S(2)}) async-start(), calls=%async_computation.2 | async-start | bytes 6291456 | tf_op jit(solution)/shard_map/all_gather | solution.py:64
  9.4 4.5 %copy-start.3 = (s32[256,1]{0,1:T(1,128)S(1)}, s32[256,1]{0,1:T(1,128)}, u32[]{:S(2)}) copy-start(s32[256,1]{0,1:T(1,128)} %param.8) | copy-start | bytes 3076
  20.6 1.3 copy-start.1
  23.7 46.4 %all-to-all-start = ((bf16[128,4,1024]{2,1,0:T(4,128)(2,1)}), bf16[128,4,1024]{2,1,0:T(4,128)(2,1)S(1)}, u32[]{:S(2)}, u32[]{:S(2)}) async-start(bf16[128,4,1024]{2,1,0:T(4,128)(2,1)} %reshape.75), calls=%async_computation | async-start | bytes 2097152 | tf_op jit(solution)/shard_map/all_to_all | solution.py:83
  71.2 4.8 %copy-start.2 = (bf16[512,8,128]{2,1,0:T(8,128)(2,1)S(1)}, bf16[512,8,128]{2,1,0:T(8,128)(2,1)}, u32[]{:S(2)}) copy-start(bf16[512,8,128]{2,1,0:T(8,128)(2,1)} %reshape_reshape.3) | copy-start | bytes 3145732
  89.7 37.1 %all-to-all-start.1 = ((bf16[128,4,1024]{2,1,0:T(4,128)(2,1)}), bf16[128,4,1024]{2,1,0:T(4,128)(2,1)}, u32[]{:S(2)}, u32[]{:S(2)}) async-start(bf16[128,4,1024]{2,1,0:T(4,128)(2,1)} %convert_element_type.71), calls=%async_computation.1 | async-start | bytes 2097152 | tf_op jit(solution)/shard_map/all_to_all | solution.py:86
  128.1 2.3 %copy-start.5 = (bf16[256,1024]{1,0:T(8,128)(2,1)S(1)}, bf16[256,1024]{1,0:T(8,128)(2,1)}, u32[]{:S(2)}) copy-start(bf16[256,1024]{1,0:T(8,128)(2,1)} %param.7) | copy-start | bytes 1572868
Sparse Core Ops, SparseCore 0:
  14.0 21.5 all-gather.1
where the time goes:
time: 140 us
  waiting for transfers between devices  58 us (41%)
  matrix products  26 us (19%)
  starting transfers between devices  22.7 us (16%)
  local copies, waits for them, and re-layouts  16.5 us (12%)
  between operations  14.2 us (10%)
  other arithmetic  2.44 us (2%)
    all_to_all x1, waiting for transfers between devices, per_device(): lax.all_to_all(outgoing, 'serve', split_axis=0, concat_axis=0, tiled=True)  30.7 us
    all_to_all x1, waiting for transfers between devices, per_device(): lax.all_to_all(partial_rows, 'serve', split_axis=0, concat_axis=0, tiled=...  27.3 us
    all_to_all x1, starting transfers between devices, per_device(): lax.all_to_all(outgoing, 'serve', split_axis=0, concat_axis=0, tiled=True)  15 us
    dot_general x1, matrix products, history_attention(): jnp.einsum('hij,jhd->ihd', weights, value_rows, preferred_element_type=jn...  10.7 us
    dot_general x2, matrix products, silu_rows(): jnp.dot(matrix, weight, preferred_element_type=jnp.float32)  10.5 us
    all_to_all x1, starting transfers between devices, per_device(): lax.all_to_all(partial_rows, 'serve', split_axis=0, concat_axis=0, tiled=...  7.69 us
    slice x1, local copies, waits for them, and re-layouts, history_attention(): key_rows = keys_vals[:, :feature_width].reshape(-1, HEADS, head_size)  4.79 us
    convert_element_type x2, local copies, waits for them, and re-layouts, history_attention(): return result.reshape(-1, feature_width).astype(jnp.bfloat16)  2.89 us
  transfers between devices with their start and end apart: 3, of which 2 were waited for; matrix products, arithmetic and copies ran while one was open for 8% of the time, Pallas kernels for 0%

commit v1 on v0

v1 whole, which is shorter than its diff:
```python
import functools
import math

import jax
import jax.numpy as jnp
from jax import lax
from jax.experimental import pallas as pl
from jax.experimental.pallas import tpu as pltpu
from jax.sharding import PartitionSpec as P

HEADS = 8
CAP = 4
BF16 = jnp.bfloat16
F32 = jnp.float32


def silu(x):
    y = 0.5 * x
    return y + y * jnp.tanh(y)


def dot(a, b):
    return jnp.dot(a, b, preferred_element_type=F32)


def weave(first, second):
    low = lax.broadcasted_iota(jnp.int32, first.shape, 1) < 4
    even = jnp.where(low, first, pltpu.roll(second, 4, 1))
    odd = jnp.where(low, pltpu.roll(first, 4, 1), second)
    return even, odd


def front_kernel(user_ref, cand_ref, w0_ref, w1_ref, out_ref, q0_ref, q1_ref, place_ref):
    rows, slots = place_ref.shape
    users = slots // CAP

    @pl.when(pl.program_id(0) == 0)
    def _():
        ids = user_ref[...]
        one_hot = jnp.where(ids == lax.broadcasted_iota(jnp.int32, (rows, users), 1), 1.0, 0.0)
        earlier = jnp.where(
            lax.broadcasted_iota(jnp.int32, (rows, rows), 1)
            < lax.broadcasted_iota(jnp.int32, (rows, rows), 0),
            1.0,
            0.0,
        )
        before = dot(earlier.astype(BF16), one_hot.astype(BF16))
        rank = jnp.sum(before * one_hot, 1, keepdims=True).astype(jnp.int32)
        slot = ids * CAP + rank
        place_ref[...] = jnp.where(
            slot == lax.broadcasted_iota(jnp.int32, (rows, slots), 1), 1.0, 0.0
        ).astype(BF16)

    place = place_ref[...]
    cand = cand_ref[...]
    parts = []
    for w_ref, q_ref in ((w0_ref, q0_ref), (w1_ref, q1_ref)):
        query = silu(dot(cand, w_ref[...])).astype(BF16)
        q_ref[...] = query
        moved = lax.dot_general(place, query, (((0,), (0,)), ((), ())), preferred_element_type=F32)
        parts.append(moved.reshape(slots // 8, 8, query.shape[1]))
    even, odd = weave(*parts)
    out_ref[:, 0] = even.astype(BF16)
    out_ref[:, 1] = odd.astype(BF16)


def front(cand_user, candidates, w_uvqk, users):
    rows, width = candidates.shape
    half = width // 2
    block = min(256, half)
    steps = half // block
    base = 2 * width // block
    slots = users * CAP
    return pl.pallas_call(
        front_kernel,
        grid=(steps,),
        in_specs=[
            pl.BlockSpec((rows, 1), lambda j: (0, 0)),
            pl.BlockSpec((rows, width), lambda j: (0, 0)),
            pl.BlockSpec((width, block), lambda j: (0, base + j)),
            pl.BlockSpec((width, block), lambda j: (0, base + steps + j)),
        ],
        out_specs=[
            pl.BlockSpec((slots // 8, 2, 8, block), lambda j: (0, 0, 0, j)),
            pl.BlockSpec((rows, block), lambda j: (0, j)),
            pl.BlockSpec((rows, block), lambda j: (0, j)),
            pl.BlockSpec((rows, slots), lambda j: (0, 0)),
        ],
        out_shape=[
            jax.ShapeDtypeStruct((slots // 8, 2, 8, half), BF16),
            jax.ShapeDtypeStruct((rows, half), BF16),
            jax.ShapeDtypeStruct((rows, half), BF16),
            jax.ShapeDtypeStruct((rows, slots), BF16),
        ],
        compiler_params=pltpu.CompilerParams(vmem_limit_bytes=40 << 20),
        cost_estimate=pl.CostEstimate(
            flops=2 * rows * width * (width + slots), bytes_accessed=5 << 20, transcendentals=rows * width
        ),
        name="front",
    )(cand_user, candidates, w_uvqk, w_uvqk)


def keys_vals_kernel(steps, info_ref, own_ref, other_ref, w_ref, out_ref):
    count = own_ref.shape[0]
    is_value = pl.program_id(0) >= steps
    weight = w_ref[...]
    for part, ref in enumerate((own_ref, other_ref)):
        start = jnp.where(info_ref[1] == part, 0, count)
        result = silu(dot(ref[...], weight))
        event = start + lax.broadcasted_iota(jnp.int32, result.shape, 0)
        keep = jnp.logical_or(jnp.logical_not(is_value), event < info_ref[0])
        out_ref[part * count : (part + 1) * count] = jnp.where(keep, result, 0.0).astype(BF16)


def keys_vals(info, own, other, w_uvqk):
    count, width = own.shape
    block = min(256, width)
    steps = width // block
    return pl.pallas_call(
        functools.partial(keys_vals_kernel, steps),
        grid=(2 * steps,),
        in_specs=[
            pl.BlockSpec(memory_space=pltpu.SMEM),
            pl.BlockSpec((count, width), lambda j: (0, 0)),
            pl.BlockSpec((count, width), lambda j: (0, 0)),
            pl.BlockSpec((width, block), lambda j: (0, jnp.where(j < steps, 3 * steps + j, j))),
        ],
        out_specs=pl.BlockSpec((2 * count, block), lambda j: (0, j)),
        out_shape=jax.ShapeDtypeStruct((2 * count, 2 * width), BF16),
        compiler_params=pltpu.CompilerParams(vmem_limit_bytes=40 << 20),
        cost_estimate=pl.CostEstimate(
            flops=8 * count * width * width, bytes_accessed=10 << 20, transcendentals=4 * count * width
        ),
        name="keys_vals",
    )(info, own, other, w_uvqk)


def attention_kernel(head_size, got_ref, key_ref, value_ref, out_ref, query_ref, result_ref):
    step = pl.program_id(0)
    steps = pl.num_programs(0)
    tiles, _, _, half = got_ref.shape
    slots = tiles * 8
    heads_half = half // head_size

    @pl.when(step == 0)
    def _():
        parts = weave(got_ref[:, 0].astype(F32), got_ref[:, 1].astype(F32))
        for index, part in enumerate(parts):
            rows = part.reshape(slots, half).astype(BF16)
            for head in range(heads_half):
                query_ref[index * heads_half + head] = rows[
                    :, head * head_size : (head + 1) * head_size
                ]

    scale = 0.5 / math.sqrt(head_size)
    chunk = min(256, slots)
    for start in range(0, slots, chunk):
        scores = lax.dot_general(
            query_ref[step, start : start + chunk],
            key_ref[...],
            (((1,), (1,)), ((), ())),
            preferred_element_type=F32,
        )
        y = scores * scale
        weights = (y + y * jnp.tanh(y)).astype(BF16)
        result_ref[step, start : start + chunk] = dot(weights, value_ref[...])

    @pl.when(step == steps - 1)
    def _():
        for head in range(heads_half):
            first = result_ref[head].reshape(tiles, 8, head_size)
            second = result_ref[heads_half + head].reshape(tiles, 8, head_size)
            even, odd = weave(first, second)
            columns = slice(head * head_size, (head + 1) * head_size)
            out_ref[:, 0, :, columns] = even.astype(BF16)
            out_ref[:, 1, :, columns] = odd.astype(BF16)


def attention(got, kv):
    tiles, _, _, half = got.shape
    slots = tiles * 8
    events = kv.shape[0]
    head_size = 2 * half // HEADS
    whole = pl.BlockSpec(got.shape, lambda h: (0, 0, 0, 0))
    return pl.pallas_call(
        functools.partial(attention_kernel, head_size),
        grid=(HEADS,),
        in_specs=[
            whole,
            pl.BlockSpec((events, head_size), lambda h: (0, h)),
            pl.BlockSpec((events, head_size), lambda h: (0, HEADS + h)),
        ],
        out_specs=whole,
        out_shape=jax.ShapeDtypeStruct(got.shape, BF16),
        scratch_shapes=[
            pltpu.VMEM((HEADS, slots, head_size), BF16),
            pltpu.VMEM((HEADS, slots, head_size), F32),
        ],
        compiler_params=pltpu.CompilerParams(vmem_limit_bytes=40 << 20),
        cost_estimate=pl.CostEstimate(
            flops=8 * slots * events * half,
            bytes_accessed=6 << 20,
            transcendentals=slots * events * HEADS,
        ),
        name="attention",
    )(got, kv, kv)


def own_kernel(head_size, cand_ref, query_ref, wg_ref, wv_ref, wk_ref, gate_ref, term_ref):
    cand = cand_ref[...]
    gate_ref[...] = silu(dot(cand, wg_ref[...])).astype(BF16)
    value = silu(dot(cand, wv_ref[...])).astype(BF16).astype(F32)
    key = silu(dot(cand, wk_ref[...])).astype(BF16).astype(F32)
    product = query_ref[...].astype(F32) * key
    for start in range(0, product.shape[1], head_size):
        columns = slice(start, start + head_size)
        score = jnp.sum(product[:, columns], 1, keepdims=True) / math.sqrt(head_size)
        term_ref[:, columns] = silu(score) * value[:, columns]


def own_part(candidates, query, w_uvqk, index):
    rows, width = candidates.shape
    half = width // 2
    block = min(256, half)
    steps = half // block
    full = width // block
    offset = index * steps
    return pl.pallas_call(
        functools.partial(own_kernel, width // HEADS),
        grid=(steps,),
        in_specs=[
            pl.BlockSpec((rows, width), lambda j: (0, 0)),
            pl.BlockSpec((rows, block), lambda j: (0, j)),
            pl.BlockSpec((width, block), lambda j: (0, offset + j)),
            pl.BlockSpec((width, block), lambda j: (0, full + offset + j)),
            pl.BlockSpec((width, block), lambda j: (0, 3 * full + offset + j)),
        ],
        out_specs=[
            pl.BlockSpec((rows, block), lambda j: (0, j)),
            pl.BlockSpec((rows, block), lambda j: (0, j)),
        ],
        out_shape=[
            jax.ShapeDtypeStruct((rows, half), BF16),
            jax.ShapeDtypeStruct((rows, half), F32),
        ],
        compiler_params=pltpu.CompilerParams(vmem_limit_bytes=40 << 20),
        cost_estimate=pl.CostEstimate(
            flops=6 * rows * width * half, bytes_accessed=5 << 20, transcendentals=3 * rows * half
        ),
        name="own_part",
    )(candidates, query, w_uvqk, w_uvqk, w_uvqk)


def tail_kernel(
    got_ref, place_ref, gate0_ref, gate1_ref, term0_ref, term1_ref, cand_ref, w_ref, out_ref, normed_ref
):
    tiles, _, _, half = got_ref.shape
    width = 2 * half

    @pl.when(pl.program_id(0) == 0)
    def _():
        place = place_ref[...]
        parts = weave(got_ref[:, 0].astype(F32), got_ref[:, 1].astype(F32))
        attended = []
        for part, term_ref in zip(parts, (term0_ref, term1_ref)):
            history = dot(place, part.reshape(tiles * 8, half).astype(BF16))
            attended.append(history + term_ref[...])
        mean = sum(jnp.sum(a, 1, keepdims=True) for a in attended) / width
        centred = [a - mean for a in attended]
        var = sum(jnp.sum(c * c, 1, keepdims=True) for c in centred) / width
        inverse = lax.rsqrt(var + 1e-05)
        for index, gate_ref in enumerate((gate0_ref, gate1_ref)):
            normed = centred[index] * inverse * gate_ref[...].astype(F32)
            normed_ref[:, index * half : (index + 1) * half] = normed.astype(BF16)

    out_ref[...] = (cand_ref[...].astype(F32) + dot(normed_ref[...], w_ref[...])).astype(BF16)


def tail(got, place, gates, terms, candidates, w_out):
    rows, width = candidates.shape
    half = width // 2
    block = min(256, width)

    def fixed(array):
        zeros = (0,) * array.ndim
        return pl.BlockSpec(array.shape, lambda j: zeros)

    return pl.pallas_call(
        tail_kernel,
        grid=(width // block,),
        in_specs=[
            fixed(got),
            fixed(place),
            fixed(gates[0]),
            fixed(gates[1]),
            fixed(terms[0]),
            fixed(terms[1]),
            pl.BlockSpec((rows, block), lambda j: (0, j)),
            pl.BlockSpec((width, block), lambda j: (0, j)),
        ],
        out_specs=pl.BlockSpec((rows, block), lambda j: (0, j)),
        out_shape=jax.ShapeDtypeStruct((rows, width), BF16),
        scratch_shapes=[pltpu.VMEM((rows, width), BF16)],
        compiler_params=pltpu.CompilerParams(vmem_limit_bytes=40 << 20),
        cost_estimate=pl.CostEstimate(
            flops=2 * rows * width * (width + got.shape[0] * 8), bytes_accessed=6 << 20, transcendentals=rows
        ),
        name="tail",
    )(got, place, *gates, *terms, candidates, w_out)


def exchange(rows):
    tiles, pair, eight, half = rows.shape
    flat = rows.reshape(tiles * pair, eight, half)
    return lax.all_to_all(flat, "serve", split_axis=0, concat_axis=0, tiled=True).reshape(rows.shape)


def per_device(history, candidates, cand_user, hist_len, w_uvqk, w_out):
    users = lax.axis_size("serve")
    outgoing, query0, query1, place = front(cand_user, candidates, w_uvqk, users)
    other = lax.ppermute(history, "rep", [(0, 1), (1, 0)])
    outgoing, history, query0, query1 = lax.optimization_barrier((outgoing, history, query0, query1))
    received = exchange(outgoing)
    info = jnp.concatenate([hist_len, lax.axis_index("rep").astype(jnp.int32)[None]])
    kv = keys_vals(info, history, other, w_uvqk)
    pairs = [own_part(candidates, query, w_uvqk, index) for index, query in enumerate((query0, query1))]
    gates, terms = [pair[0] for pair in pairs], [pair[1] for pair in pairs]
    returned = exchange(attention(received, kv))
    return tail(returned, place, gates, terms, candidates, w_out)


def solution(mesh):
    placed = (
        P(("serve", "rep"), None),
        P(("serve", "rep"), None),
        P(("serve", "rep"), None),
        P("serve"),
        P(),
        P(),
    )
    return jax.shard_map(
        per_device, mesh=mesh, in_specs=placed, out_specs=P(("serve", "rep"), None), check_vma=False
    )
```

time: 140 us -> 111 us (0.79)
  Pallas kernels: 0 us -> 30.6 us
  matrix products: 26 us -> 0 us
  waiting for transfers between devices: 58 us -> 39.7 us
  between operations: 14.2 us -> 0.76 us
  other arithmetic: 2.44 us -> 0.08 us
    pallas_call x0 -> x6, Pallas kernels: none -> 30.6 us  [the longest x1 9.82 us: attention(): pl.pallas_call(functools.partial(attention_kernel, head_size), grid=(HEAD...]
    dot_general x6 -> x0, matrix products: 26 us -> none  [the longest x1 10.7 us: history_attention(): jnp.einsum('hij,jhd->ihd', weights, value_rows, preferred_element_type=jn...]
    all_to_all x2, waiting for transfers between devices: 58 us -> 37.4 us  [exchange(): lax.all_to_all(flat, 'serve', split_axis=0, concat_axis=0, tiled=True)]
    unnamed x14 -> x21, local copies, waits for them, and re-layouts: 1.55 us -> 17.2 us
    slice x2 -> x0, local copies, waits for them, and re-layouts: 7.61 us -> none  [the longest x1 4.79 us: history_attention(): key_rows = keys_vals[:, :feature_width].reshape(-1, HEADS, head_size)]
    convert_element_type x2 -> x0, local copies, waits for them, and re-layouts: 2.89 us -> none  [history_attention(): return result.reshape(-1, feature_width).astype(jnp.bfloat16)]
    reshape x2 -> x0, local copies, waits for them, and re-layouts: 2.63 us -> none  [the longest x1 1.34 us: per_device(): returned.reshape(-1, feature_width)]
    ppermute x0 -> x1, waiting for transfers between devices: none -> 2.26 us  [per_device(): other = lax.ppermute(history, 'rep', [(0, 1), (1, 0)])]
  transfers between devices with their start and end apart: 3 -> 3, of which waited for: 2 -> 3; matrix products, arithmetic and copies ran while one was open for 8% -> 0% of each run, Pallas kernels for 0% -> 12%
where the time goes in v1:
time: 111 us; the launch traced here: 110 us
  waiting for transfers between devices  39.7 us (36%)
  Pallas kernels  30.6 us (28%)
  starting transfers between devices  21.7 us (20%)
  local copies, waits for them, and re-layouts  17.2 us (15%)
    all_to_all x2, waiting for transfers between devices, exchange(): lax.all_to_all(flat, 'serve', split_axis=0, concat_axis=0, tiled=True)  37.4 us
    all_to_all x2, starting transfers between devices, exchange(): lax.all_to_all(flat, 'serve', split_axis=0, concat_axis=0, tiled=True)  21.6 us
    unnamed x21, local copies, waits for them, and re-layouts  17.2 us
    pallas_call x1, Pallas kernels, attention(): pl.pallas_call(functools.partial(attention_kernel, head_size), grid=(HEAD...  9.82 us
    pallas_call x1, Pallas kernels, keys_vals(): pl.pallas_call(functools.partial(keys_vals_kernel, steps), grid=(2 * step...  9.23 us
    pallas_call x2, Pallas kernels, own_part(): pl.pallas_call(functools.partial(own_kernel, width // HEADS), grid=(steps...  4.11 us
    pallas_call x1, Pallas kernels, front(): pl.pallas_call(front_kernel, grid=(steps,), in_specs=[pl.BlockSpec((rows,...  4.04 us
    pallas_call x1, Pallas kernels, tail(): pl.pallas_call(tail_kernel, grid=(width // block,), in_specs=[fixed(got),...  3.39 us
  transfers between devices with their start and end apart: 3, of which 3 were waited for; matrix products, arithmetic and copies ran while one was open for 0% of the time, Pallas kernels for 12%

profile of v1, /device:TPU:32, one launch (start us, length us, event | category | flops | bytes accessed | tf_op | source)
XLA Modules:
  0.0 110.0 jit_solution(10630784367162457943)
XLA Ops:
  0.0 0.8 copy.7.user_ref
  0.8 3.4 %copy-done = bf16[1024,4096]{1,0:T(8,128)(2,1)S(1)} copy-done((bf16[1024,4096]{1,0:T(8,128)(2,1)S(1)}, bf16[1024,4096]{1,0:T(8,128)(2,1)}, u32[]{:S(2)}) %copy-start) | copy-done | bytes 8388632
  4.2 1.0 copy-done.4
  5.2 4.0 %front.1 = (bf16[64,2,8,512]{3,2,1,0:T(8,128)(2,1)}, bf16[256,512]{1,0:T(8,128)(2,1)S(1)}, bf16[256,512]{1,0:T(8,128)(2,1)S(1)}, bf16[256,512]{1,0:T(8,128)(2,1)S(1)}) custom-call(s32[256,1]{1,0:T(8,128)S(1)} %copy.7.user_ref, bf16[256,1024]{1,0:T(8,128)(2,1)S(1)} %copy-done.4, bf16[1024,4096]{1,0:T(8,128)(2,1)S(1)} %copy-done, bf16[1024,4096]{1,0:T(8,128)(2,1)S(1)} %copy-done), custom_call_target="tpu_custom_call" | custom-call | flops 805306368 | bytes 5242880 | tf_op jit(solution)/shard_map/front/pallas_call | solution.py:74
  9.3 15.0 %all-to-all-start = ((bf16[128,8,512]{2,1,0:T(8,128)(2,1)}), bf16[128,8,512]{2,1,0:T(8,128)(2,1)S(1)}, u32[]{:S(2)}, u32[]{:S(2)}) async-start(bf16[128,8,512]{2,1,0:T(8,128)(2,1)} %bitcast), calls=%async_computation | async-start | bytes 2097152 | tf_op jit(solution)/shard_map/all_to_all | solution.py:315
  24.3 0.1 collective-permute-start
  25.0 0.1 pad_add_fusion.info_ref
  25.1 2.3 %collective-permute-done.other_ref = bf16[512,1024]{1,0:T(8,128)(2,1)} collective-permute-done((bf16[512,1024]{1,0:T(8,128)(2,1)}, bf16[512,1024]{1,0:T(8,128)(2,1)}, u32[]{:S(2)}, u32[]{:S(2)}) %collective-permute-start) | collective-permute-done | bytes 1048608 | tf_op jit(solution)/shard_map/ppermute | solution.py:321
  27.4 1.2 %copy-done.9 = bf16[512,1024]{1,0:T(8,128)(2,1)S(1)} copy-done((bf16[512,1024]{1,0:T(8,128)(2,1)S(1)}, bf16[512,1024]{1,0:T(8,128)(2,1)}, u32[]{:S(2)}) %copy-start.9) | copy-done | bytes 1048600
  28.6 9.2 %keys_vals.1.key_ref.value_ref = bf16[1024,2048]{1,0:T(8,128)(2,1)S(1)} custom-call(s32[2]{0:T(128)S(1)} %pad_add_fusion.info_ref, bf16[512,1024]{1,0:T(8,128)(2,1)S(1)} %copy-done.9, bf16[512,1024]{1,0:T(8,128)(2,1)} %collective-permute-done.other_ref, bf16[1024,4096]{1,0:T(8,128)(2,1)} %wk_ref.3), custom_call_target="tpu_custom_call" | custom-call | flops 4294967296 | bytes 10485760 | tf_op jit(solution)/shard_map/keys_vals/pallas_call | solution.py:119
  37.9 2.0 %copy-done.2 = bf16[1024,2048]{1,0:T(8,128)(2,1)} copy-done((bf16[1024,2048]{1,0:T(8,128)(2,1)}, bf16[1024,2048]{1,0:T(8,128)(2,1)S(1)}, u32[]{:S(2)}) %copy-start.2) | copy-done | bytes 4194328
  39.8 15.8 %all-to-all-done = bf16[128,8,512]{2,1,0:T(8,128)(2,1)S(1)} async-done(((bf16[128,8,512]{2,1,0:T(8,128)(2,1)}), bf16[128,8,512]{2,1,0:T(8,128)(2,1)S(1)}, u32[]{:S(2)}, u32[]{:S(2)}) %all-to-all-start) | async-done | bytes 1048608 | tf_op jit(solution)/shard_map/all_to_all | solution.py:315
  55.7 2.2 %copy-done.3 = bf16[1024,2048]{1,0:T(8,128)(2,1)S(1)} copy-done((bf16[1024,2048]{1,0:T(8,128)(2,1)S(1)}, bf16[1024,2048]{1,0:T(8,128)(2,1)}, u32[]{:S(2)}) %copy-start.3) | copy-done | bytes 4194328
  57.8 9.8 %attention.1 = bf16[64,2,8,512]{3,2,1,0:T(8,128)(2,1)} custom-call(bf16[64,2,8,512]{3,2,1,0:T(8,128)(2,1)S(1)} %bitcast.5, bf16[1024,2048]{1,0:T(8,128)(2,1)S(1)} %copy-done.3, bf16[1024,2048]{1,0:T(8,128)(2,1)S(1)} %copy-done.3), custom_call_target="tpu_custom_call" | custom-call | flops 2147483648 | bytes 6291456 | tf_op jit(solution)/shard_map/attention/pallas_call | solution.py:185
  67.7 6.6 %all-to-all-start.1 = ((bf16[128,8,512]{2,1,0:T(8,128)(2,1)}), bf16[128,8,512]{2,1,0:T(8,128)(2,1)S(1)}, u32[]{:S(2)}, u32[]{:S(2)}) async-start(bf16[128,8,512]{2,1,0:T(8,128)(2,1)} %bitcast.3), calls=%async_computation.1 | async-start | bytes 2097152 | tf_op jit(solution)/shard_map/all_to_all | solution.py:315
  74.3 0.0 copy-start.1
  74.3 3.4 %copy-done.1 = bf16[1024,4096]{1,0:T(8,128)(2,1)S(1)} copy-done((bf16[1024,4096]{1,0:T(8,128)(2,1)S(1)}, bf16[1024,4096]{1,0:T(8,128)(2,1)}, u32[]{:S(2)}) %copy-start.1) | copy-done | bytes 8388632
  77.7 2.0 %own_part.2 = (bf16[256,512]{1,0:T(8,128)(2,1)S(1)}, f32[256,512]{1,0:T(8,128)S(1)}) custom-call(bf16[256,1024]{1,0:T(8,128)(2,1)S(1)} %copy-done.5, bf16[256,512]{1,0:T(8,128)(2,1)S(1)} %get-tuple-element.23.query_ref, bf16[1024,4096]{1,0:T(8,128)(2,1)S(1)} %copy-done.1, bf16[1024,4096]{1,0:T(8,128)(2,1)S(1)} %copy-done.1, bf16[1024,4096]{1,0:T(8,128)(2,1)S(1)} %copy-done.1), custom_call_target="tpu_custom_call" | custom-call | flops 805306368 | bytes 5242880 | tf_op jit(solution)/shard_map/own_part/pallas_call | solution.py:228
  79.8 2.1 %own_part.3 = (bf16[256,512]{1,0:T(8,128)(2,1)S(1)}, f32[256,512]{1,0:T(8,128)S(1)}) custom-call(bf16[256,1024]{1,0:T(8,128)(2,1)S(1)} %copy-done.5, bf16[256,512]{1,0:T(8,128)(2,1)S(1)} %get-tuple-element.25.query_ref, bf16[1024,4096]{1,0:T(8,128)(2,1)S(1)} %copy-done.1, bf16[1024,4096]{1,0:T(8,128)(2,1)S(1)} %copy-done.1, bf16[1024,4096]{1,0:T(8,128)(2,1)S(1)} %copy-done.1), custom_call_target="tpu_custom_call" | custom-call | flops 805306368 | bytes 5242880 | tf_op jit(solution)/shard_map/own_part/pallas_call | solution.py:228
  81.8 0.7 copy-done.7
  82.5 21.6 %all-to-all-done.1 = bf16[128,8,512]{2,1,0:T(8,128)(2,1)S(1)} async-done(((bf16[128,8,512]{2,1,0:T(8,128)(2,1)}), bf16[128,8,512]{2,1,0:T(8,128)(2,1)S(1)}, u32[]{:S(2)}, u32[]{:S(2)}) %all-to-all-start.1) | async-done | bytes 1048608 | tf_op jit(solution)/shard_map/all_to_all | solution.py:315
  104.1 1.6 %copy-done.6 = bf16[1024,1024]{1,0:T(8,128)(2,1)S(1)} copy-done((bf16[1024,1024]{1,0:T(8,128)(2,1)S(1)}, bf16[1024,1024]{1,0:T(8,128)(2,1)}, u32[]{:S(2)}) %copy-start.6) | copy-done | bytes 2097176
  105.7 0.9 copy-done.8
  106.6 3.4 %tail.1 = bf16[256,1024]{1,0:T(8,128)(2,1)} custom-call(bf16[64,2,8,512]{3,2,1,0:T(8,128)(2,1)S(1)} %bitcast.6, bf16[256,512]{1,0:T(8,128)(2,1)S(1)} %get-tuple-element.22.place_ref, bf16[256,512]{1,0:T(8,128)(2,1)S(1)} %get-tuple-element.24.gate0_ref, bf16[256,512]{1,0:T(8,128)(2,1)S(1)} %copy-done.8, f32[256,512]{1,0:T(8,128)S(1)} %get-tuple-element.27.term0_ref, ...), custom_call_target="tpu_custom_call" | custom-call | flops 805306368 | bytes 6291456 | tf_op jit(solution)/shard_map/tail/pallas_call | solution.py:288
  (10 shorter events, 0.0 us)
Async XLA Ops:
  0.8 3.4 %copy-start = (bf16[1024,4096]{1,0:T(8,128)(2,1)S(1)}, bf16[1024,4096]{1,0:T(8,128)(2,1)}, u32[]{:S(2)}) copy-start(bf16[1024,4096]{1,0:T(8,128)(2,1)} %wk_ref.3) | copy-start | bytes 25165828
  4.2 1.0 copy-start.4
  9.3 46.4 %all-to-all-start = ((bf16[128,8,512]{2,1,0:T(8,128)(2,1)}), bf16[128,8,512]{2,1,0:T(8,128)(2,1)S(1)}, u32[]{:S(2)}, u32[]{:S(2)}) async-start(bf16[128,8,512]{2,1,0:T(8,128)(2,1)} %bitcast), calls=%async_computation | async-start | bytes 2097152 | tf_op jit(solution)/shard_map/all_to_all | solution.py:315
  24.3 3.1 %collective-permute-start = (bf16[512,1024]{1,0:T(8,128)(2,1)}, bf16[512,1024]{1,0:T(8,128)(2,1)}, u32[]{:S(2)}, u32[]{:S(2)}) collective-permute-start(bf16[512,1024]{1,0:T(8,128)(2,1)} %own_ref), channel_id=1, source_target_pairs={{0,1},{1,0},{2,3},{3,2},{4,5},{5,4},{6,7},{7,6},{8,9},{9,8},{10,11... | collective-permute-start | bytes 3145736 | tf_op jit(solution)/shard_map/ppermute | solution.py:321
  27.4 1.2 %copy-start.9 = (bf16[512,1024]{1,0:T(8,128)(2,1)S(1)}, bf16[512,1024]{1,0:T(8,128)(2,1)}, u32[]{:S(2)}) copy-start(bf16[512,1024]{1,0:T(8,128)(2,1)} %own_ref) | copy-start | bytes 3145732
  37.8 2.0 %copy-start.2 = (bf16[1024,2048]{1,0:T(8,128)(2,1)}, bf16[1024,2048]{1,0:T(8,128)(2,1)S(1)}, u32[]{:S(2)}) copy-start(bf16[1024,2048]{1,0:T(8,128)(2,1)S(1)} %keys_vals.1.key_ref.value_ref) | copy-start | bytes 12582916
  55.7 2.2 %copy-start.3 = (bf16[1024,2048]{1,0:T(8,128)(2,1)S(1)}, bf16[1024,2048]{1,0:T(8,128)(2,1)}, u32[]{:S(2)}) copy-start(bf16[1024,2048]{1,0:T(8,128)(2,1)} %copy-done.2) | copy-start | bytes 12582916
  57.8 16.5 %copy-start.5 = (bf16[256,1024]{1,0:T(8,128)(2,1)S(1)}, bf16[256,1024]{1,0:T(8,128)(2,1)}, u32[]{:S(2)}) copy-start(bf16[256,1024]{1,0:T(8,128)(2,1)} %cand_ref.7) | copy-start | bytes 1572868
  67.7 36.4 %all-to-all-start.1 = ((bf16[128,8,512]{2,1,0:T(8,128)(2,1)}), bf16[128,8,512]{2,1,0:T(8,128)(2,1)S(1)}, u32[]{:S(2)}, u32[]{:S(2)}) async-start(bf16[128,8,512]{2,1,0:T(8,128)(2,1)} %bitcast.3), calls=%async_computation.1 | async-start | bytes 2097152 | tf_op jit(solution)/shard_map/all_to_all | solution.py:315
  74.3 3.4 %copy-start.1 = (bf16[1024,4096]{1,0:T(8,128)(2,1)S(1)}, bf16[1024,4096]{1,0:T(8,128)(2,1)}, u32[]{:S(2)}) copy-start(bf16[1024,4096]{1,0:T(8,128)(2,1)} %wk_ref.3) | copy-start | bytes 25165828
  81.8 0.7 copy-start.7
  104.1 1.6 %copy-start.6 = (bf16[1024,1024]{1,0:T(8,128)(2,1)S(1)}, bf16[1024,1024]{1,0:T(8,128)(2,1)}, u32[]{:S(2)}) copy-start(bf16[1024,1024]{1,0:T(8,128)(2,1)} %w_ref.3) | copy-start | bytes 6291460
  105.7 0.9 copy-start.8

commit v2 on v1

v2 whole, which is shorter than its diff:
```python
import functools
import math

import jax
import jax.numpy as jnp
from jax import lax
from jax.experimental import pallas as pl
from jax.experimental.pallas import tpu as pltpu
from jax.sharding import PartitionSpec as P

HEADS = 8
CAP = 4
FRONT_PARTS = 4
FRONT_OUTS = 2
VMEM_LIMIT = 60 << 20
BF16 = jnp.bfloat16
F32 = jnp.float32


def silu(x):
    y = 0.5 * x
    return y + y * jnp.tanh(y)


def dot(a, b):
    return jnp.dot(a, b, preferred_element_type=F32)


def weave(first, second):
    low = lax.broadcasted_iota(jnp.int32, first.shape, 1) < 4
    even = jnp.where(low, first, pltpu.roll(second, 4, 1))
    odd = jnp.where(low, pltpu.roll(first, 4, 1), second)
    return even, odd


def params():
    return pltpu.CompilerParams(vmem_limit_bytes=VMEM_LIMIT)


def front_kernel(user_ref, cand_hbm, w_hbm, out_hbm, query_ref, place_ref, cand_ref, w_ref, out_ref, in_sems, out_sems):
    slots, rows = place_ref.shape
    users = slots // CAP
    width = cand_ref.shape[1]
    half = width // 2
    parts = w_ref.shape[0]
    depth = width // parts
    copies = [pltpu.make_async_copy(cand_hbm, cand_ref, in_sems.at[parts])]
    for index in range(parts):
        source = w_hbm.at[pl.ds(index * depth, depth), pl.ds(2 * width, width)]
        copies.append(pltpu.make_async_copy(source, w_ref.at[index], in_sems.at[index]))
    for copy in copies:
        copy.start()

    ids = user_ref[...]
    one_hot = jnp.where(ids == lax.broadcasted_iota(jnp.int32, (users, rows), 0), 1.0, 0.0)
    earlier = jnp.where(
        lax.broadcasted_iota(jnp.int32, (rows, rows), 0)
        < lax.broadcasted_iota(jnp.int32, (rows, rows), 1),
        1.0,
        0.0,
    )
    before = dot(one_hot.astype(BF16), earlier.astype(BF16))
    rank = jnp.sum(before * one_hot, 0, keepdims=True).astype(jnp.int32)
    slot = ids * CAP + rank
    place = jnp.where(slot == lax.broadcasted_iota(jnp.int32, (slots, rows), 0), 1.0, 0.0).astype(BF16)
    place_ref[...] = place

    copies[0].wait()
    total = None
    for index in range(parts):
        copies[1 + index].wait()
        term = dot(cand_ref[:, index * depth : (index + 1) * depth], w_ref[index])
        total = term if total is None else total + term
    query = silu(total).astype(BF16)
    query_ref[...] = query
    block = half // out_sems.shape[0]
    outs = []
    for index in range(half // block):
        pair = []
        for start in (index * block, half + index * block):
            moved = dot(place, query[:, start : start + block])
            pair.append(moved.reshape(slots // 8, 8, block))
        even, odd = weave(*pair)
        columns = pl.ds(index * block, block)
        out_ref[:, 0, :, columns] = even.astype(BF16)
        out_ref[:, 1, :, columns] = odd.astype(BF16)
        copy = pltpu.make_async_copy(
            out_ref.at[:, :, :, columns], out_hbm.at[:, :, :, columns], out_sems.at[index]
        )
        copy.start()
        outs.append(copy)
    for copy in outs:
        copy.wait()


def front(cand_user, candidates, w_uvqk, users):
    rows, width = candidates.shape
    half = width // 2
    slots = users * CAP
    parts = FRONT_PARTS
    whole = pl.BlockSpec(memory_space=pl.ANY)
    inside = pl.BlockSpec(memory_space=pltpu.VMEM)
    tiles = (slots // 8, 2, 8, half)
    return pl.pallas_call(
        front_kernel,
        in_specs=[inside, whole, whole],
        out_specs=[whole, inside, inside],
        out_shape=[
            jax.ShapeDtypeStruct(tiles, BF16),
            jax.ShapeDtypeStruct((rows, width), BF16),
            jax.ShapeDtypeStruct((slots, rows), BF16),
        ],
        scratch_shapes=[
            pltpu.VMEM((rows, width), BF16),
            pltpu.VMEM((parts, width // parts, width), BF16),
            pltpu.VMEM(tiles, BF16),
            pltpu.SemaphoreType.DMA((parts + 1,)),
            pltpu.SemaphoreType.DMA((FRONT_OUTS,)),
        ],
        compiler_params=params(),
        cost_estimate=pl.CostEstimate(
            flops=2 * rows * width * (width + slots), bytes_accessed=5 << 20, transcendentals=rows * width
        ),
        name="front",
    )(cand_user.reshape(1, rows), candidates, w_uvqk)


def keys_vals_kernel(steps, info_ref, own_ref, other_ref, w_ref, key_ref, value_ref):
    count = own_ref.shape[0]
    weight = w_ref[...]
    for part, ref in enumerate((own_ref, other_ref)):
        result = silu(dot(ref[...], weight))
        span = slice(part * count, (part + 1) * count)

        @pl.when(pl.program_id(0) < steps)
        def _():
            key_ref[:, span] = result.T.astype(BF16)

        @pl.when(pl.program_id(0) >= steps)
        def _():
            start = jnp.where(info_ref[1] == part, 0, count)
            event = start + lax.broadcasted_iota(jnp.int32, result.shape, 0)
            value = jnp.where(event < info_ref[0], result, 0.0).astype(BF16)
            head_size = value_ref.shape[2]
            for head in range(value_ref.shape[0]):
                value_ref[head, span] = value[:, head * head_size : (head + 1) * head_size]


def keys_vals(info, own, other, w_uvqk):
    count, width = own.shape
    block = min(256, width)
    steps = width // block
    return pl.pallas_call(
        functools.partial(keys_vals_kernel, steps),
        grid=(2 * steps,),
        in_specs=[
            pl.BlockSpec(memory_space=pltpu.SMEM),
            pl.BlockSpec((count, width), lambda j: (0, 0)),
            pl.BlockSpec((count, width), lambda j: (0, 0)),
            pl.BlockSpec((width, block), lambda j: (0, jnp.where(j < steps, 3 * steps + j, j))),
        ],
        out_specs=[
            pl.BlockSpec((block, 2 * count), lambda j: (jnp.minimum(j, steps - 1), 0)),
            pl.BlockSpec((HEADS // steps, 2 * count, width // HEADS), lambda j: (jnp.maximum(j - steps, 0), 0, 0)),
        ],
        out_shape=[
            jax.ShapeDtypeStruct((width, 2 * count), BF16),
            jax.ShapeDtypeStruct((HEADS, 2 * count, width // HEADS), BF16),
        ],
        compiler_params=params(),
        cost_estimate=pl.CostEstimate(
            flops=8 * count * width * width, bytes_accessed=10 << 20, transcendentals=4 * count * width
        ),
        name="keys_vals",
    )(info, own, other, w_uvqk)


def attention_kernel(got_hbm, key_hbm, value_hbm, out_hbm, got_ref, key_ref, value_ref, out_ref, in_sems, out_sems):
    tiles, _, _, half = got_ref.shape
    slots = tiles * 8
    head_size = 2 * half // HEADS
    pairs = HEADS // 2
    got_copy = pltpu.make_async_copy(got_hbm, got_ref, in_sems.at[2 * HEADS])
    got_copy.start()
    copies = {}
    for pair in range(pairs):
        for head in (pair, pairs + pair):
            rows = pl.ds(head * head_size, head_size)
            copies[head] = (
                pltpu.make_async_copy(key_hbm.at[rows], key_ref.at[head], in_sems.at[head]),
                pltpu.make_async_copy(value_hbm.at[head], value_ref.at[head], in_sems.at[HEADS + head]),
            )
            for copy in copies[head]:
                copy.start()
    scale = 0.5 / math.sqrt(head_size)
    got_copy.wait()
    outs = []
    for pair in range(pairs):
        columns = pl.ds(pair * head_size, head_size)
        for head in (pair, pairs + pair):
            for copy in copies[head]:
                copy.wait()
        queries = weave(got_ref[:, 0, :, columns].astype(F32), got_ref[:, 1, :, columns].astype(F32))
        results = []
        for query, head in zip(queries, (pair, pairs + pair)):
            rows = query.reshape(slots, head_size).astype(BF16)
            y = dot(rows, key_ref[head]) * scale
            weights = (y + y * jnp.tanh(y)).astype(BF16)
            results.append(dot(weights, value_ref[head]).reshape(tiles, 8, head_size))
        even, odd = weave(*results)
        out_ref[:, 0, :, columns] = even.astype(BF16)
        out_ref[:, 1, :, columns] = odd.astype(BF16)
        copy = pltpu.make_async_copy(
            out_ref.at[:, :, :, columns], out_hbm.at[:, :, :, columns], out_sems.at[pair]
        )
        copy.start()
        outs.append(copy)
    for copy in outs:
        copy.wait()


def attention(got, keys, values):
    tiles, _, _, half = got.shape
    slots = tiles * 8
    heads, events, head_size = values.shape
    whole = pl.BlockSpec(memory_space=pl.ANY)
    return pl.pallas_call(
        attention_kernel,
        in_specs=[whole] * 3,
        out_specs=whole,
        out_shape=jax.ShapeDtypeStruct(got.shape, BF16),
        scratch_shapes=[
            pltpu.VMEM(got.shape, BF16),
            pltpu.VMEM((heads, head_size, events), BF16),
            pltpu.VMEM((heads, events, head_size), BF16),
            pltpu.VMEM(got.shape, BF16),
            pltpu.SemaphoreType.DMA((2 * heads + 1,)),
            pltpu.SemaphoreType.DMA((heads // 2,)),
        ],
        compiler_params=params(),
        cost_estimate=pl.CostEstimate(
            flops=8 * slots * events * half,
            bytes_accessed=6 << 20,
            transcendentals=slots * events * heads,
        ),
        name="attention",
    )(got, keys, values)


def own_kernel(head_size, cand_ref, query_ref, wg_ref, wv_ref, wk_ref, place_ref, gate_ref, term_ref, turned_ref):
    @pl.when(pl.program_id(0) == 0)
    def _():
        turned_ref[...] = place_ref[...].astype(F32).T.astype(BF16)

    cand = cand_ref[...]
    gate_ref[...] = silu(dot(cand, wg_ref[...])).astype(BF16)
    value = silu(dot(cand, wv_ref[...])).astype(BF16).astype(F32)
    key = silu(dot(cand, wk_ref[...])).astype(BF16).astype(F32)
    product = query_ref[...].astype(F32) * key
    for start in range(0, product.shape[1], head_size):
        columns = slice(start, start + head_size)
        score = jnp.sum(product[:, columns], 1, keepdims=True) / math.sqrt(head_size)
        term_ref[:, columns] = silu(score) * value[:, columns]


def own_part(candidates, query, w_uvqk, place):
    rows, width = candidates.shape
    slots = place.shape[0]
    block = 256
    steps = width // block
    column = pl.BlockSpec((rows, block), lambda j: (0, j))
    return pl.pallas_call(
        functools.partial(own_kernel, width // HEADS),
        grid=(steps,),
        in_specs=[
            pl.BlockSpec((rows, width), lambda j: (0, 0)),
            column,
            pl.BlockSpec((width, block), lambda j: (0, j)),
            pl.BlockSpec((width, block), lambda j: (0, steps + j)),
            pl.BlockSpec((width, block), lambda j: (0, 3 * steps + j)),
            pl.BlockSpec((slots, rows), lambda j: (0, 0)),
        ],
        out_specs=[column, column, pl.BlockSpec((rows, slots), lambda j: (0, 0))],
        out_shape=[
            jax.ShapeDtypeStruct((rows, width), BF16),
            jax.ShapeDtypeStruct((rows, width), F32),
            jax.ShapeDtypeStruct((rows, slots), BF16),
        ],
        compiler_params=params(),
        cost_estimate=pl.CostEstimate(
            flops=6 * rows * width * width, bytes_accessed=9 << 20, transcendentals=3 * rows * width
        ),
        name="own_part",
    )(candidates, query, w_uvqk, w_uvqk, w_uvqk, place)


def tail_kernel(*refs):
    sources, out_hbm = refs[:6], refs[6]
    buffers, out_ref = refs[7:13], refs[13]
    in_sems, out_sems = refs[14], refs[15]
    copies = [
        pltpu.make_async_copy(source, buffer, in_sems.at[index])
        for index, (source, buffer) in enumerate(zip(sources, buffers))
    ]
    for copy in copies:
        copy.start()
    place_ref, got_ref, term_ref, gate_ref, w_ref, cand_ref = buffers
    tiles, _, _, half = got_ref.shape
    width = 2 * half
    copies[0].wait()
    copies[1].wait()
    place = place_ref[...]
    parts = weave(got_ref[:, 0].astype(F32), got_ref[:, 1].astype(F32))
    history = [dot(place, part.reshape(tiles * 8, half).astype(BF16)) for part in parts]
    copies[2].wait()
    attended = jnp.concatenate(history, 1) + term_ref[...]
    mean = jnp.sum(attended, 1, keepdims=True) / width
    centred = attended - mean
    var = jnp.sum(centred * centred, 1, keepdims=True) / width
    scaled = centred * lax.rsqrt(var + 1e-05)
    copies[3].wait()
    normed = (scaled * gate_ref[...].astype(F32)).astype(BF16)
    copies[4].wait()
    copies[5].wait()
    block = 256
    outs = []
    for index in range(width // block):
        columns = slice(index * block, (index + 1) * block)
        result = cand_ref[:, columns].astype(F32) + dot(normed, w_ref[:, columns])
        out_ref[:, columns] = result.astype(BF16)
        copy = pltpu.make_async_copy(
            out_ref.at[:, pl.ds(index * block, block)],
            out_hbm.at[:, pl.ds(index * block, block)],
            out_sems.at[index],
        )
        copy.start()
        outs.append(copy)
    for copy in outs:
        copy.wait()


def tail(got, place, gate, term, candidates, w_out):
    rows, width = candidates.shape
    sources = (place, got, term, gate, w_out, candidates)
    return pl.pallas_call(
        tail_kernel,
        in_specs=[pl.BlockSpec(memory_space=pl.ANY)] * 6,
        out_specs=pl.BlockSpec(memory_space=pl.ANY),
        out_shape=jax.ShapeDtypeStruct((rows, width), BF16),
        scratch_shapes=[pltpu.VMEM(source.shape, source.dtype) for source in sources]
        + [
            pltpu.VMEM((rows, width), BF16),
            pltpu.SemaphoreType.DMA((6,)),
            pltpu.SemaphoreType.DMA((width // 256,)),
        ],
        compiler_params=params(),
        cost_estimate=pl.CostEstimate(
            flops=2 * rows * width * (width + got.shape[0] * 8), bytes_accessed=6 << 20, transcendentals=rows
        ),
        name="tail",
    )(*sources)


def exchange(rows):
    tiles, pair, eight, half = rows.shape
    flat = rows.reshape(tiles * pair, eight, half)
    return lax.all_to_all(flat, "serve", split_axis=0, concat_axis=0, tiled=True).reshape(rows.shape)


def per_device(history, candidates, cand_user, hist_len, w_uvqk, w_out):
    users = lax.axis_size("serve")
    outgoing, query, place = front(cand_user, candidates, w_uvqk, users)
    other = lax.ppermute(history, "rep", [(0, 1), (1, 0)])
    outgoing, history, query = lax.optimization_barrier((outgoing, history, query))
    received = exchange(outgoing)
    info = jnp.concatenate([hist_len, lax.axis_index("rep").astype(jnp.int32)[None]])
    keys, values = keys_vals(info, history, other, w_uvqk)
    gate, term, turned = own_part(candidates, query, w_uvqk, place)
    returned = exchange(attention(received, keys, values))
    return tail(returned, turned, gate, term, candidates, w_out)


def solution(mesh):
    placed = (
        P(("serve", "rep"), None),
        P(("serve", "rep"), None),
        P(("serve", "rep"), None),
        P("serve"),
        P(),
        P(),
    )
    return jax.shard_map(
        per_device, mesh=mesh, in_specs=placed, out_specs=P(("serve", "rep"), None), check_vma=False
    )
```

time: 111 us -> 103 us (0.928)
  local copies, waits for them, and re-layouts: 17.2 us -> 2.99 us
  Pallas kernels: 30.6 us -> 39.5 us
  waiting for transfers between devices: 39.7 us -> 36.3 us
    unnamed x21 -> x8, local copies, waits for them, and re-layouts: 17.2 us -> 2.99 us
    pallas_call x1, Pallas kernels: 9.23 us -> 15.9 us  [keys_vals(): pl.pallas_call(functools.partial(keys_vals_kernel, steps), grid=(2 * step...]
    pallas_call x2 -> x1, Pallas kernels: 4.11 us -> 6.61 us  [own_part(): pl.pallas_call(functools.partial(own_kernel, width // HEADS), grid=(steps...]
    all_to_all x2, waiting for transfers between devices: 37.4 us -> 34.9 us  [exchange(): lax.all_to_all(flat, 'serve', split_axis=0, concat_axis=0, tiled=True)]
  transfers between devices with their start and end apart: 3 -> 3, of which waited for: 3 -> 3; matrix products, arithmetic and copies ran while one was open for 0% -> 1% of each run, Pallas kernels for 12% -> 22%
where the time goes in v2:
time: 103 us; the launch traced here: 102 us
  Pallas kernels  39.5 us (38%)
  waiting for transfers between devices  36.3 us (35%)
  starting transfers between devices  22.1 us (21%)
  local copies, waits for them, and re-layouts  2.99 us (3%)
    all_to_all x2, waiting for transfers between devices, exchange(): lax.all_to_all(flat, 'serve', split_axis=0, concat_axis=0, tiled=True)  34.9 us
    all_to_all x2, starting transfers between devices, exchange(): lax.all_to_all(flat, 'serve', split_axis=0, concat_axis=0, tiled=True)  22 us
    pallas_call x1, Pallas kernels, keys_vals(): pl.pallas_call(functools.partial(keys_vals_kernel, steps), grid=(2 * step...  15.9 us
    pallas_call x1, Pallas kernels, attention(): pl.pallas_call(attention_kernel, in_specs=[whole] * 3, out_specs=whole, o...  7.92 us
    pallas_call x1, Pallas kernels, own_part(): pl.pallas_call(functools.partial(own_kernel, width // HEADS), grid=(steps...  6.61 us
    pallas_call x1, Pallas kernels, front(): pl.pallas_call(front_kernel, in_specs=[inside, whole, whole], out_specs=[...  5.1 us
    pallas_call x1, Pallas kernels, tail(): pl.pallas_call(tail_kernel, in_specs=[pl.BlockSpec(memory_space=pl.ANY)]...  4.06 us
    unnamed x8, local copies, waits for them, and re-layouts  2.99 us
  transfers between devices with their start and end apart: 3, of which 3 were waited for; matrix products, arithmetic and copies ran while one was open for 1% of the time, Pallas kernels for 22%

profile of v2, /device:TPU:32, one launch (start us, length us, event | category | flops | bytes accessed | tf_op | source)
XLA Modules:
  0.0 102.4 jit_solution(4423944439164780863)
XLA Ops:
  0.0 5.1 %front.1 = (bf16[64,2,8,512]{3,2,1,0:T(8,128)(2,1)}, bf16[256,1024]{1,0:T(8,128)(2,1)}, bf16[512,256]{1,0:T(8,128)(2,1)}) custom-call(s32[1,256]{1,0:T(1,128)} %bitcast.10, bf16[256,1024]{1,0:T(8,128)(2,1)} %refs_5_.1, bf16[1024,4096]{1,0:T(8,128)(2,1)} %w_ref.1), custom_call_target="tpu_custom_call" | custom-call | flops 805306368 | bytes 5242880 | tf_op jit(solution)/shard_map/front/pallas_call | solution.py:104
  5.1 0.0 copy-start.2
  5.1 15.1 %all-to-all-start = ((bf16[128,8,512]{2,1,0:T(8,128)(2,1)}), bf16[128,8,512]{2,1,0:T(8,128)(2,1)S(1)}, u32[]{:S(2)}, u32[]{:S(2)}) async-start(bf16[128,8,512]{2,1,0:T(8,128)(2,1)} %bitcast.8), calls=%async_computation | async-start | bytes 2097152 | tf_op jit(solution)/shard_map/all_to_all | solution.py:367
  20.3 0.0 copy-done.2
  20.3 0.1 collective-permute-start
  21.0 0.6 pad_add_fusion.info_ref
  21.6 1.4 %collective-permute-done.other_ref = bf16[512,1024]{1,0:T(8,128)(2,1)S(1)} collective-permute-done((bf16[512,1024]{1,0:T(8,128)(2,1)S(1)}, bf16[512,1024]{1,0:T(8,128)(2,1)S(1)}, u32[]{:S(2)}, u32[]{:S(2)}) %collective-permute-start) | collective-permute-done | bytes 1048608 | tf_op jit(solution)/shard_map/ppermute | solution.py:373
  23.0 0.0 copy-start.3
  23.0 1.0 copy-done.3
  24.0 15.9 %keys_vals.1 = (bf16[1024,1024]{1,0:T(8,128)(2,1)}, bf16[8,1024,128]{2,1,0:T(8,128)(2,1)}) custom-call(s32[2]{0:T(128)} %pad_add_fusion.info_ref, bf16[512,1024]{1,0:T(8,128)(2,1)} %own_ref, bf16[512,1024]{1,0:T(8,128)(2,1)} %copy-done.3, bf16[1024,4096]{1,0:T(8,128)(2,1)} %w_ref.1), custom_call_target="tpu_custom_call" | custom-call | flops 4294967296 | bytes 10485760 | tf_op jit(solution)/shard_map/keys_vals/pallas_call | solution.py:153
  39.9 11.7 %all-to-all-done = bf16[128,8,512]{2,1,0:T(8,128)(2,1)S(1)} async-done(((bf16[128,8,512]{2,1,0:T(8,128)(2,1)}), bf16[128,8,512]{2,1,0:T(8,128)(2,1)S(1)}, u32[]{:S(2)}, u32[]{:S(2)}) %all-to-all-start) | async-done | bytes 1048608 | tf_op jit(solution)/shard_map/all_to_all | solution.py:367
  51.6 0.0 copy-start.1
  51.6 1.0 copy-done.1
  52.6 7.9 %attention.1 = bf16[64,2,8,512]{3,2,1,0:T(8,128)(2,1)} custom-call(bf16[64,2,8,512]{3,2,1,0:T(8,128)(2,1)} %bitcast.7, bf16[1024,1024]{1,0:T(8,128)(2,1)} %get-tuple-element.23.key_hbm, bf16[8,1024,128]{2,1,0:T(8,128)(2,1)} %get-tuple-element.24.value_hbm), custom_call_target="tpu_custom_call" | custom-call | flops 2147483648 | bytes 6291456 | tf_op jit(solution)/shard_map/attention/pallas_call | solution.py:227
  60.6 6.8 %all-to-all-start.1 = ((bf16[128,8,512]{2,1,0:T(8,128)(2,1)}), bf16[128,8,512]{2,1,0:T(8,128)(2,1)S(1)}, u32[]{:S(2)}, u32[]{:S(2)}) async-start(bf16[128,8,512]{2,1,0:T(8,128)(2,1)} %bitcast.9), calls=%async_computation.1 | async-start | bytes 2097152 | tf_op jit(solution)/shard_map/all_to_all | solution.py:367
  67.4 6.6 %own_part.1 = (bf16[256,1024]{1,0:T(8,128)(2,1)}, f32[256,1024]{1,0:T(8,128)}, bf16[256,512]{1,0:T(8,128)(2,1)}) custom-call(bf16[256,1024]{1,0:T(8,128)(2,1)} %refs_5_.1, bf16[256,1024]{1,0:T(8,128)(2,1)} %get-tuple-element.18.query_ref, bf16[1024,4096]{1,0:T(8,128)(2,1)} %w_ref.1, bf16[1024,4096]{1,0:T(8,128)(2,1)} %w_ref.1, bf16[1024,4096]{1,0:T(8,128)(2,1)} %w_ref.1, ...), custom_call_target="tpu_custom_call" | custom-call | flops 1610612736 | bytes 9437184 | tf_op jit(solution)/shard_map/own_part/pallas_call | solution.py:272
  74.0 23.2 %all-to-all-done.1 = bf16[128,8,512]{2,1,0:T(8,128)(2,1)S(1)} async-done(((bf16[128,8,512]{2,1,0:T(8,128)(2,1)}), bf16[128,8,512]{2,1,0:T(8,128)(2,1)S(1)}, u32[]{:S(2)}, u32[]{:S(2)}) %all-to-all-start.1) | async-done | bytes 1048608 | tf_op jit(solution)/shard_map/all_to_all | solution.py:367
  97.2 0.0 copy-start
  97.2 1.0 copy-done
  98.2 4.1 %tail.1 = bf16[256,1024]{1,0:T(8,128)(2,1)} custom-call(bf16[256,512]{1,0:T(8,128)(2,1)} %get-tuple-element.20.refs_0_, bf16[64,2,8,512]{3,2,1,0:T(8,128)(2,1)} %bitcast.6, f32[256,1024]{1,0:T(8,128)} %get-tuple-element.25.refs_2_, bf16[256,1024]{1,0:T(8,128)(2,1)} %get-tuple-element.26.refs_3_, bf16[1024,1024]{1,0:T(8,128)(2,1)} %refs_4_.1, ...), custom_call_target="tpu_custom_call" | custom-call | flops 805306368 | bytes 6291456 | tf_op jit(solution)/shard_map/tail/pallas_call | solution.py:345
Async XLA Ops:
  5.1 15.2 %copy-start.2 = (bf16[512,1024]{1,0:T(8,128)(2,1)S(1)}, bf16[512,1024]{1,0:T(8,128)(2,1)}, u32[]{:S(2)}) copy-start(bf16[512,1024]{1,0:T(8,128)(2,1)} %own_ref) | copy-start | bytes 3145732
  5.1 46.5 %all-to-all-start = ((bf16[128,8,512]{2,1,0:T(8,128)(2,1)}), bf16[128,8,512]{2,1,0:T(8,128)(2,1)S(1)}, u32[]{:S(2)}, u32[]{:S(2)}) async-start(bf16[128,8,512]{2,1,0:T(8,128)(2,1)} %bitcast.8), calls=%async_computation | async-start | bytes 2097152 | tf_op jit(solution)/shard_map/all_to_all | solution.py:367
  20.3 2.7 %collective-permute-start = (bf16[512,1024]{1,0:T(8,128)(2,1)S(1)}, bf16[512,1024]{1,0:T(8,128)(2,1)S(1)}, u32[]{:S(2)}, u32[]{:S(2)}) collective-permute-start(bf16[512,1024]{1,0:T(8,128)(2,1)S(1)} %copy-done.2), channel_id=1, source_target_pairs={{0,1},{1,0},{2,3},{3,2},{4,5},{5,4},{6,7},{7,6},{8,9},{9,8},{10,11... | collective-permute-start | bytes 3145736 | tf_op jit(solution)/shard_map/ppermute | solution.py:373
  23.0 1.0 copy-start.3
  51.6 1.0 copy-start.1
  60.6 36.6 %all-to-all-start.1 = ((bf16[128,8,512]{2,1,0:T(8,128)(2,1)}), bf16[128,8,512]{2,1,0:T(8,128)(2,1)S(1)}, u32[]{:S(2)}, u32[]{:S(2)}) async-start(bf16[128,8,512]{2,1,0:T(8,128)(2,1)} %bitcast.9), calls=%async_computation.1 | async-start | bytes 2097152 | tf_op jit(solution)/shard_map/all_to_all | solution.py:367
  97.2 1.0 copy-start

commit v3 on v2

--- a/solution.py
+++ b/solution.py
@@ -10,9 +10,6 @@
 
 HEADS = 8
 CAP = 4
-FRONT_PARTS = 4
-FRONT_OUTS = 2
-VMEM_LIMIT = 60 << 20
 BF16 = jnp.bfloat16
 F32 = jnp.float32
 
@@ -24,6 +21,11 @@
 
 def dot(a, b):
     return jnp.dot(a, b, preferred_element_type=F32)
+
+
+def turn(matrix, identity):
+    turned = lax.dot_general(matrix, identity, (((0,), (0,)), ((), ())), preferred_element_type=F32)
+    return turned.astype(BF16)
 
 
 def weave(first, second):
@@ -33,24 +35,30 @@
     return even, odd
 
 
-def params():
-    return pltpu.CompilerParams(vmem_limit_bytes=VMEM_LIMIT)
-
-
-def front_kernel(user_ref, cand_hbm, w_hbm, out_hbm, query_ref, place_ref, cand_ref, w_ref, out_ref, in_sems, out_sems):
+def params(limit=60):
+    return pltpu.CompilerParams(vmem_limit_bytes=limit << 20)
+
+
+def front_kernel(
+    user_hbm, cand_hbm, w_hbm, out_hbm, place_hbm, user_ref, cand_ref, w_ref, out_ref, place_ref, in_sems, out_sems
+):
     slots, rows = place_ref.shape
     users = slots // CAP
     width = cand_ref.shape[1]
-    half = width // 2
-    parts = w_ref.shape[0]
-    depth = width // parts
-    copies = [pltpu.make_async_copy(cand_hbm, cand_ref, in_sems.at[parts])]
-    for index in range(parts):
-        source = w_hbm.at[pl.ds(index * depth, depth), pl.ds(2 * width, width)]
-        copies.append(pltpu.make_async_copy(source, w_ref.at[index], in_sems.at[index]))
+    parts, _, block = w_ref.shape
+    steps = parts // 2
+    copies = [
+        pltpu.make_async_copy(user_hbm, user_ref, in_sems.at[0]),
+        pltpu.make_async_copy(cand_hbm, cand_ref, in_sems.at[1]),
+    ]
+    for index in range(steps):
+        for part in (index, steps + index):
+            source = w_hbm.at[:, pl.ds(2 * width + part * block, block)]
+            copies.append(pltpu.make_async_copy(source, w_ref.at[part], in_sems.at[2 + part]))
     for copy in copies:
         copy.start()
 
+    copies[0].wait()
     ids = user_ref[...]
     one_hot = jnp.where(ids == lax.broadcasted_iota(jnp.int32, (users, rows), 0), 1.0, 0.0)
     earlier = jnp.where(
@@ -64,28 +72,22 @@
     slot = ids * CAP + rank
     place = jnp.where(slot == lax.broadcasted_iota(jnp.int32, (slots, rows), 0), 1.0, 0.0).astype(BF16)
     place_ref[...] = place
-
-    copies[0].wait()
-    total = None
-    for index in range(parts):
-        copies[1 + index].wait()
-        term = dot(cand_ref[:, index * depth : (index + 1) * depth], w_ref[index])
-        total = term if total is None else total + term
-    query = silu(total).astype(BF16)
-    query_ref[...] = query
-    block = half // out_sems.shape[0]
-    outs = []
-    for index in range(half // block):
+    outs = [pltpu.make_async_copy(place_ref, place_hbm, out_sems.at[0])]
+    outs[0].start()
+
+    copies[1].wait()
+    for index in range(steps):
         pair = []
-        for start in (index * block, half + index * block):
-            moved = dot(place, query[:, start : start + block])
-            pair.append(moved.reshape(slots // 8, 8, block))
+        for offset, part in enumerate((index, steps + index)):
+            copies[2 + 2 * index + offset].wait()
+            query = silu(dot(cand_ref[...], w_ref[part])).astype(BF16)
+            pair.append(dot(place, query).reshape(slots // 8, 8, block))
         even, odd = weave(*pair)
         columns = pl.ds(index * block, block)
         out_ref[:, 0, :, columns] = even.astype(BF16)
         out_ref[:, 1, :, columns] = odd.astype(BF16)
         copy = pltpu.make_async_copy(
-            out_ref.at[:, :, :, columns], out_hbm.at[:, :, :, columns], out_sems.at[index]
+            out_ref.at[:, :, :, columns], out_hbm.at[:, :, :, columns], out_sems.at[1 + index]
         )
         copy.start()
         outs.append(copy)
@@ -97,25 +99,26 @@
     rows, width = candidates.shape
     half = width // 2
     slots = users * CAP
-    parts = FRONT_PARTS
+    block = 256
+    parts = width // block
     whole = pl.BlockSpec(memory_space=pl.ANY)
-    inside = pl.BlockSpec(memory_space=pltpu.VMEM)
     tiles = (slots // 8, 2, 8, half)
     return pl.pallas_call(
         front_kernel,
-        in_specs=[inside, whole, whole],
-        out_specs=[whole, inside, inside],
+        in_specs=[whole] * 3,
+        out_specs=[whole] * 2,
         out_shape=[
             jax.ShapeDtypeStruct(tiles, BF16),
-            jax.ShapeDtypeStruct((rows, width), BF16),
             jax.ShapeDtypeStruct((slots, rows), BF16),
         ],
         scratch_shapes=[
+            pltpu.VMEM((1, rows), jnp.int32),
             pltpu.VMEM((rows, width), BF16),
-            pltpu.VMEM((parts, width // parts, width), BF16),
+            pltpu.VMEM((parts, width, block), BF16),
             pltpu.VMEM(tiles, BF16),
-            pltpu.SemaphoreType.DMA((parts + 1,)),
-            pltpu.SemaphoreType.DMA((FRONT_OUTS,)),
+            pltpu.VMEM((slots, rows), BF16),
+            pltpu.SemaphoreType.DMA((parts + 2,)),
+            pltpu.SemaphoreType.DMA((parts // 2 + 1,)),
         ],
         compiler_params=params(),
         cost_estimate=pl.CostEstimate(
@@ -134,7 +137,10 @@
 
         @pl.when(pl.program_id(0) < steps)
         def _():
-            key_ref[:, span] = result.T.astype(BF16)
+            row = lax.broadcasted_iota(jnp.int32, (count, count), 0)
+            column = lax.broadcasted_iota(jnp.int32, (count, count), 1)
+            identity = jnp.where(row == column, 1.0, 0.0).astype(BF16)
+            key_ref[:, span] = turn(result.astype(BF16), identity)
 
         @pl.when(pl.program_id(0) >= steps)
         def _():
@@ -237,7 +243,7 @@
             pltpu.SemaphoreType.DMA((2 * heads + 1,)),
             pltpu.SemaphoreType.DMA((heads // 2,)),
         ],
-        compiler_params=params(),
+        compiler_params=params(50),
         cost_estimate=pl.CostEstimate(
             flops=8 * slots * events * half,
             bytes_accessed=6 << 20,
@@ -247,104 +253,113 @@
     )(got, keys, values)
 
 
-def own_kernel(head_size, cand_ref, query_ref, wg_ref, wv_ref, wk_ref, place_ref, gate_ref, term_ref, turned_ref):
-    @pl.when(pl.program_id(0) == 0)
+def own_kernel(head_size, cand_ref, wg_ref, wv_ref, wq_ref, wk_ref, place_ref, out_ref):
+    step = pl.program_id(0)
+    block = wg_ref.shape[1]
+    rows, width = cand_ref.shape
+    slots = place_ref.shape[0]
+
+    @pl.when(step == 0)
     def _():
-        turned_ref[...] = place_ref[...].astype(F32).T.astype(BF16)
+        out_ref[:, 3 * width : 3 * width + slots] = place_ref[...].astype(F32).T.astype(BF16)
 
     cand = cand_ref[...]
-    gate_ref[...] = silu(dot(cand, wg_ref[...])).astype(BF16)
-    value = silu(dot(cand, wv_ref[...])).astype(BF16).astype(F32)
-    key = silu(dot(cand, wk_ref[...])).astype(BF16).astype(F32)
-    product = query_ref[...].astype(F32) * key
-    for start in range(0, product.shape[1], head_size):
+    gate, value, query, key = (
+        silu(dot(cand, ref[...])).astype(BF16) for ref in (wg_ref, wv_ref, wq_ref, wk_ref)
+    )
+    product = query.astype(F32) * key.astype(F32)
+    value = value.astype(F32)
+    terms = []
+    for start in range(0, block, head_size):
         columns = slice(start, start + head_size)
         score = jnp.sum(product[:, columns], 1, keepdims=True) / math.sqrt(head_size)
-        term_ref[:, columns] = silu(score) * value[:, columns]
-
-
-def own_part(candidates, query, w_uvqk, place):
+        terms.append(silu(score) * value[:, columns])
+    term = jnp.concatenate(terms, 1)
+    high = term.astype(BF16)
+    low = (term - high.astype(F32)).astype(BF16)
+    for index, array in enumerate((high, low, gate)):
+        start = pl.multiple_of(index * width + step * block, block)
+        out_ref[:, pl.ds(start, block)] = array
+
+
+def own_part(candidates, w_uvqk, place):
     rows, width = candidates.shape
     slots = place.shape[0]
     block = 256
     steps = width // block
-    column = pl.BlockSpec((rows, block), lambda j: (0, j))
     return pl.pallas_call(
         functools.partial(own_kernel, width // HEADS),
         grid=(steps,),
         in_specs=[
             pl.BlockSpec((rows, width), lambda j: (0, 0)),
-            column,
             pl.BlockSpec((width, block), lambda j: (0, j)),
             pl.BlockSpec((width, block), lambda j: (0, steps + j)),
+            pl.BlockSpec((width, block), lambda j: (0, 2 * steps + j)),
             pl.BlockSpec((width, block), lambda j: (0, 3 * steps + j)),
             pl.BlockSpec((slots, rows), lambda j: (0, 0)),
         ],
-        out_specs=[column, column, pl.BlockSpec((rows, slots), lambda j: (0, 0))],
-        out_shape=[
-            jax.ShapeDtypeStruct((rows, width), BF16),
-            jax.ShapeDtypeStruct((rows, width), F32),
-            jax.ShapeDtypeStruct((rows, slots), BF16),
-        ],
+        out_specs=pl.BlockSpec((rows, 3 * width + slots), lambda j: (0, 0)),
+        out_shape=jax.ShapeDtypeStruct((rows, 3 * width + slots), BF16),
         compiler_params=params(),
         cost_estimate=pl.CostEstimate(
-            flops=6 * rows * width * width, bytes_accessed=9 << 20, transcendentals=3 * rows * width
+            flops=8 * rows * width * width, bytes_accessed=11 << 20, transcendentals=4 * rows * width
         ),
         name="own_part",
-    )(candidates, query, w_uvqk, w_uvqk, w_uvqk, place)
-
-
-def tail_kernel(*refs):
-    sources, out_hbm = refs[:6], refs[6]
-    buffers, out_ref = refs[7:13], refs[13]
-    in_sems, out_sems = refs[14], refs[15]
-    copies = [
-        pltpu.make_async_copy(source, buffer, in_sems.at[index])
-        for index, (source, buffer) in enumerate(zip(sources, buffers))
-    ]
-    for copy in copies:
-        copy.start()
-    place_ref, got_ref, term_ref, gate_ref, w_ref, cand_ref = buffers
+    )(candidates, w_uvqk, w_uvqk, w_uvqk, w_uvqk, place)
+
+
+def tail_kernel(
+    got_hbm, own_hbm, cand_hbm, w_hbm, out_hbm, got_ref, own_ref, cand_ref, w_ref, out_ref, in_sems, out_sems
+):
     tiles, _, _, half = got_ref.shape
     width = 2 * half
-    copies[0].wait()
-    copies[1].wait()
-    place = place_ref[...]
+    slots = tiles * 8
+    spans = (pl.ds(3 * width, slots), pl.ds(0, 2 * width), pl.ds(2 * width, width))
+    got_copy = pltpu.make_async_copy(got_hbm, got_ref, in_sems.at[0])
+    place_copy, term_copy, gate_copy = (
+        pltpu.make_async_copy(own_hbm.at[:, span], own_ref.at[:, span], in_sems.at[1 + index])
+        for index, span in enumerate(spans)
+    )
+    w_copy = pltpu.make_async_copy(w_hbm, w_ref, in_sems.at[4])
+    cand_copy = pltpu.make_async_copy(cand_hbm, cand_ref, in_sems.at[5])
+    for copy in (got_copy, place_copy, term_copy, gate_copy, w_copy, cand_copy):
+        copy.start()
+    got_copy.wait()
+    place_copy.wait()
+    place = own_ref[:, 3 * width : 3 * width + slots]
     parts = weave(got_ref[:, 0].astype(F32), got_ref[:, 1].astype(F32))
-    history = [dot(place, part.reshape(tiles * 8, half).astype(BF16)) for part in parts]
-    copies[2].wait()
-    attended = jnp.concatenate(history, 1) + term_ref[...]
+    history = [dot(place, part.reshape(slots, half).astype(BF16)) for part in parts]
+    term_copy.wait()
+    term = own_ref[:, :width].astype(F32) + own_ref[:, width : 2 * width].astype(F32)
+    attended = jnp.concatenate(history, 1) + term
     mean = jnp.sum(attended, 1, keepdims=True) / width
     centred = attended - mean
     var = jnp.sum(centred * centred, 1, keepdims=True) / width
     scaled = centred * lax.rsqrt(var + 1e-05)
-    copies[3].wait()
-    normed = (scaled * gate_ref[...].astype(F32)).astype(BF16)
-    copies[4].wait()
-    copies[5].wait()
+    gate_copy.wait()
+    normed = (scaled * own_ref[:, 2 * width : 3 * width].astype(F32)).astype(BF16)
+    w_copy.wait()
+    cand_copy.wait()
     block = 256
     outs = []
     for index in range(width // block):
         columns = slice(index * block, (index + 1) * block)
         result = cand_ref[:, columns].astype(F32) + dot(normed, w_ref[:, columns])
         out_ref[:, columns] = result.astype(BF16)
-        copy = pltpu.make_async_copy(
-            out_ref.at[:, pl.ds(index * block, block)],
-            out_hbm.at[:, pl.ds(index * block, block)],
-            out_sems.at[index],
-        )
+        span = pl.ds(index * block, block)
+        copy = pltpu.make_async_copy(out_ref.at[:, span], out_hbm.at[:, span], out_sems.at[index])
         copy.start()
         outs.append(copy)
     for copy in outs:
         copy.wait()
 
 
-def tail(got, place, gate, term, candidates, w_out):
+def tail(got, own, candidates, w_out):
     rows, width = candidates.shape
-    sources = (place, got, term, gate, w_out, candidates)
+    sources = (got, own, candidates, w_out)
     return pl.pallas_call(
         tail_kernel,
-        in_specs=[pl.BlockSpec(memory_space=pl.ANY)] * 6,
+        in_specs=[pl.BlockSpec(memory_space=pl.ANY)] * 4,
         out_specs=pl.BlockSpec(memory_space=pl.ANY),
         out_shape=jax.ShapeDtypeStruct((rows, width), BF16),
         scratch_shapes=[pltpu.VMEM(source.shape, source.dtype) for source in sources]
@@ -353,7 +368,7 @@
             pltpu.SemaphoreType.DMA((6,)),
             pltpu.SemaphoreType.DMA((width // 256,)),
         ],
-        compiler_params=params(),
+        compiler_params=params(51),
         cost_estimate=pl.CostEstimate(
             flops=2 * rows * width * (width + got.shape[0] * 8), bytes_accessed=6 << 20, transcendentals=rows
         ),
@@ -369,15 +384,15 @@
 
 def per_device(history, candidates, cand_user, hist_len, w_uvqk, w_out):
     users = lax.axis_size("serve")
-    outgoing, query, place = front(cand_user, candidates, w_uvqk, users)
+    outgoing, place = front(cand_user, candidates, w_uvqk, users)
     other = lax.ppermute(history, "rep", [(0, 1), (1, 0)])
-    outgoing, history, query = lax.optimization_barrier((outgoing, history, query))
+    outgoing, history, place = lax.optimization_barrier((outgoing, history, place))
     received = exchange(outgoing)
     info = jnp.concatenate([hist_len, lax.axis_index("rep").astype(jnp.int32)[None]])
     keys, values = keys_vals(info, history, other, w_uvqk)
-    gate, term, turned = own_part(candidates, query, w_uvqk, place)
+    own = own_part(candidates, w_uvqk, place)
     returned = exchange(attention(received, keys, values))
-    return tail(returned, turned, gate, term, candidates, w_out)
+    return tail(returned, own, candidates, w_out)
 
 
 def solution(mesh):

time: 103 us -> 100 us (0.971)
  local copies, waits for them, and re-layouts: 2.99 us -> 1.01 us
  Pallas kernels: 39.5 us -> 37.8 us
    pallas_call x1, Pallas kernels: 15.9 us -> 13.7 us  [keys_vals(): pl.pallas_call(functools.partial(keys_vals_kernel, steps), grid=(2 * step...]
    unnamed x8 -> x6, local copies, waits for them, and re-layouts: 2.99 us -> 1.01 us
    pallas_call x1, Pallas kernels: 6.61 us -> 7.86 us  [own_part(): pl.pallas_call(functools.partial(own_kernel, width // HEADS), grid=(steps...]
where the time goes in v3:
time: 100 us; the launch traced here: 99.6 us
  Pallas kernels  37.8 us (38%)
  waiting for transfers between devices  37.2 us (37%)
  starting transfers between devices  22.1 us (22%)
  local copies, waits for them, and re-layouts  1.01 us (1%)
    all_to_all x2, waiting for transfers between devices, exchange(): lax.all_to_all(flat, 'serve', split_axis=0, concat_axis=0, tiled=True)  35.8 us
    all_to_all x2, starting transfers between devices, exchange(): lax.all_to_all(flat, 'serve', split_axis=0, concat_axis=0, tiled=True)  22 us
    pallas_call x1, Pallas kernels, keys_vals(): pl.pallas_call(functools.partial(keys_vals_kernel, steps), grid=(2 * step...  13.7 us
    pallas_call x1, Pallas kernels, own_part(): pl.pallas_call(functools.partial(own_kernel, width // HEADS), grid=(steps...  7.86 us
    pallas_call x1, Pallas kernels, attention(): pl.pallas_call(attention_kernel, in_specs=[whole] * 3, out_specs=whole, o...  7.68 us
    pallas_call x1, Pallas kernels, front(): pl.pallas_call(front_kernel, in_specs=[whole] * 3, out_specs=[whole] * 2,...  4.82 us
    pallas_call x1, Pallas kernels, tail(): pl.pallas_call(tail_kernel, in_specs=[pl.BlockSpec(memory_space=pl.ANY)]...  3.75 us
  transfers between devices with their start and end apart: 3, of which 3 were waited for; matrix products, arithmetic and copies ran while one was open for 1% of the time, Pallas kernels for 22%

profile of v3, /device:TPU:32, one launch (start us, length us, event | category | flops | bytes accessed | tf_op | source)
XLA Modules:
  0.0 99.6 jit_solution(761635036252446595)
XLA Ops:
  0.0 4.8 %front.1 = (bf16[64,2,8,512]{3,2,1,0:T(8,128)(2,1)}, bf16[512,256]{1,0:T(8,128)(2,1)}) custom-call(s32[1,256]{1,0:T(1,128)} %bitcast.9, bf16[256,1024]{1,0:T(8,128)(2,1)} %cand_hbm.3, bf16[1024,4096]{1,0:T(8,128)(2,1)} %wk_ref.1), custom_call_target="tpu_custom_call" | custom-call | flops 805306368 | bytes 5242880 | tf_op jit(solution)/shard_map/front/pallas_call | solution.py:106
  4.8 0.0 copy-start.1
  4.8 15.1 %all-to-all-start = ((bf16[128,8,512]{2,1,0:T(8,128)(2,1)}), bf16[128,8,512]{2,1,0:T(8,128)(2,1)S(1)}, u32[]{:S(2)}, u32[]{:S(2)}) async-start(bf16[128,8,512]{2,1,0:T(8,128)(2,1)} %bitcast.8), calls=%async_computation | async-start | bytes 2097152 | tf_op jit(solution)/shard_map/all_to_all | solution.py:382
  20.0 0.0 copy-done.1
  20.0 0.1 collective-permute-start
  20.8 0.6 pad_add_fusion.info_ref
  21.4 1.4 %collective-permute-done.other_ref = bf16[512,1024]{1,0:T(8,128)(2,1)S(1)} collective-permute-done((bf16[512,1024]{1,0:T(8,128)(2,1)S(1)}, bf16[512,1024]{1,0:T(8,128)(2,1)S(1)}, u32[]{:S(2)}, u32[]{:S(2)}) %collective-permute-start) | collective-permute-done | bytes 1048608 | tf_op jit(solution)/shard_map/ppermute | solution.py:388
  22.8 0.0 copy-start.2
  22.8 1.0 %copy-done.2 = bf16[512,1024]{1,0:T(8,128)(2,1)} copy-done((bf16[512,1024]{1,0:T(8,128)(2,1)}, bf16[512,1024]{1,0:T(8,128)(2,1)S(1)}, u32[]{:S(2)}) %copy-start.2) | copy-done | bytes 1048600
  23.8 13.7 %keys_vals.1 = (bf16[1024,1024]{1,0:T(8,128)(2,1)}, bf16[8,1024,128]{2,1,0:T(8,128)(2,1)}) custom-call(s32[2]{0:T(128)} %pad_add_fusion.info_ref, bf16[512,1024]{1,0:T(8,128)(2,1)} %own_ref, bf16[512,1024]{1,0:T(8,128)(2,1)} %copy-done.2, bf16[1024,4096]{1,0:T(8,128)(2,1)} %wk_ref.1), custom_call_target="tpu_custom_call" | custom-call | flops 4294967296 | bytes 10485760 | tf_op jit(solution)/shard_map/keys_vals/pallas_call | solution.py:159
  37.4 13.9 %all-to-all-done = bf16[128,8,512]{2,1,0:T(8,128)(2,1)S(1)} async-done(((bf16[128,8,512]{2,1,0:T(8,128)(2,1)}), bf16[128,8,512]{2,1,0:T(8,128)(2,1)S(1)}, u32[]{:S(2)}, u32[]{:S(2)}) %all-to-all-start) | async-done | bytes 1048608 | tf_op jit(solution)/shard_map/all_to_all | solution.py:382
  51.3 7.7 %attention.1 = bf16[64,2,8,512]{3,2,1,0:T(8,128)(2,1)} custom-call(bf16[64,2,8,512]{3,2,1,0:T(8,128)(2,1)S(1)} %bitcast.7, bf16[1024,1024]{1,0:T(8,128)(2,1)} %get-tuple-element.16.key_hbm, bf16[8,1024,128]{2,1,0:T(8,128)(2,1)} %get-tuple-element.17.value_hbm), custom_call_target="tpu_custom_call" | custom-call | flops 2147483648 | bytes 6291456 | tf_op jit(solution)/shard_map/attention/pallas_call | solution.py:233
  59.0 6.8 %all-to-all-start.1 = ((bf16[128,8,512]{2,1,0:T(8,128)(2,1)}), bf16[128,8,512]{2,1,0:T(8,128)(2,1)S(1)}, u32[]{:S(2)}, u32[]{:S(2)}) async-start(bf16[128,8,512]{2,1,0:T(8,128)(2,1)} %bitcast.4), calls=%async_computation.1 | async-start | bytes 2097152 | tf_op jit(solution)/shard_map/all_to_all | solution.py:382
  65.9 0.0 copy-start
  65.9 7.9 %own_part.1.own_hbm = bf16[256,3584]{1,0:T(8,128)(2,1)} custom-call(bf16[256,1024]{1,0:T(8,128)(2,1)} %cand_hbm.3, bf16[1024,4096]{1,0:T(8,128)(2,1)} %wk_ref.1, bf16[1024,4096]{1,0:T(8,128)(2,1)} %wk_ref.1, bf16[1024,4096]{1,0:T(8,128)(2,1)} %wk_ref.1, bf16[1024,4096]{1,0:T(8,128)(2,1)} %wk_ref.1, bf16[512,256]{1,0:T(8,128)(2,1)} %get-tuple-element.18.place_ref), custom_call_target="tpu_custom_call" | custom-call | flops 2147483648 | bytes 11534336 | tf_op jit(solution)/shard_map/own_part/pallas_call | solution.py:290
  73.7 21.9 %all-to-all-done.1 = bf16[128,8,512]{2,1,0:T(8,128)(2,1)S(1)} async-done(((bf16[128,8,512]{2,1,0:T(8,128)(2,1)}), bf16[128,8,512]{2,1,0:T(8,128)(2,1)S(1)}, u32[]{:S(2)}, u32[]{:S(2)}) %all-to-all-start.1) | async-done | bytes 1048608 | tf_op jit(solution)/shard_map/all_to_all | solution.py:382
  95.7 0.0 copy-done
  95.7 3.8 %tail.1 = bf16[256,1024]{1,0:T(8,128)(2,1)} custom-call(bf16[64,2,8,512]{3,2,1,0:T(8,128)(2,1)S(1)} %bitcast.6, bf16[256,3584]{1,0:T(8,128)(2,1)} %own_part.1.own_hbm, bf16[256,1024]{1,0:T(8,128)(2,1)S(1)} %copy-done, bf16[1024,1024]{1,0:T(8,128)(2,1)} %w_hbm.3), custom_call_target="tpu_custom_call" | custom-call | flops 805306368 | bytes 6291456 | tf_op jit(solution)/shard_map/tail/pallas_call | solution.py:360
Async XLA Ops:
  4.8 15.2 %copy-start.1 = (bf16[512,1024]{1,0:T(8,128)(2,1)S(1)}, bf16[512,1024]{1,0:T(8,128)(2,1)}, u32[]{:S(2)}) copy-start(bf16[512,1024]{1,0:T(8,128)(2,1)} %own_ref) | copy-start | bytes 3145732
  4.8 46.5 %all-to-all-start = ((bf16[128,8,512]{2,1,0:T(8,128)(2,1)}), bf16[128,8,512]{2,1,0:T(8,128)(2,1)S(1)}, u32[]{:S(2)}, u32[]{:S(2)}) async-start(bf16[128,8,512]{2,1,0:T(8,128)(2,1)} %bitcast.8), calls=%async_computation | async-start | bytes 2097152 | tf_op jit(solution)/shard_map/all_to_all | solution.py:382
  20.0 2.7 %collective-permute-start = (bf16[512,1024]{1,0:T(8,128)(2,1)S(1)}, bf16[512,1024]{1,0:T(8,128)(2,1)S(1)}, u32[]{:S(2)}, u32[]{:S(2)}) collective-permute-start(bf16[512,1024]{1,0:T(8,128)(2,1)S(1)} %copy-done.1), channel_id=1, source_target_pairs={{0,1},{1,0},{2,3},{3,2},{4,5},{5,4},{6,7},{7,6},{8,9},{9,8},{10,11... | collective-permute-start | bytes 3145736 | tf_op jit(solution)/shard_map/ppermute | solution.py:388
  22.8 1.0 %copy-start.2 = (bf16[512,1024]{1,0:T(8,128)(2,1)}, bf16[512,1024]{1,0:T(8,128)(2,1)S(1)}, u32[]{:S(2)}) copy-start(bf16[512,1024]{1,0:T(8,128)(2,1)S(1)} %collective-permute-done.other_ref) | copy-start | bytes 3145732
  59.0 36.6 %all-to-all-start.1 = ((bf16[128,8,512]{2,1,0:T(8,128)(2,1)}), bf16[128,8,512]{2,1,0:T(8,128)(2,1)S(1)}, u32[]{:S(2)}, u32[]{:S(2)}) async-start(bf16[128,8,512]{2,1,0:T(8,128)(2,1)} %bitcast.4), calls=%async_computation.1 | async-start | bytes 2097152 | tf_op jit(solution)/shard_map/all_to_all | solution.py:382
  65.9 29.8 %copy-start = (bf16[256,1024]{1,0:T(8,128)(2,1)S(1)}, bf16[256,1024]{1,0:T(8,128)(2,1)}, u32[]{:S(2)}) copy-start(bf16[256,1024]{1,0:T(8,128)(2,1)} %cand_hbm.3) | copy-start | bytes 1572868

commit v4 on v3

--- a/solution.py
+++ b/solution.py
@@ -45,16 +45,14 @@
     slots, rows = place_ref.shape
     users = slots // CAP
     width = cand_ref.shape[1]
-    parts, _, block = w_ref.shape
-    steps = parts // 2
+    parts, depth, _ = w_ref.shape
     copies = [
         pltpu.make_async_copy(user_hbm, user_ref, in_sems.at[0]),
         pltpu.make_async_copy(cand_hbm, cand_ref, in_sems.at[1]),
     ]
-    for index in range(steps):
-        for part in (index, steps + index):
-            source = w_hbm.at[:, pl.ds(2 * width + part * block, block)]
-            copies.append(pltpu.make_async_copy(source, w_ref.at[part], in_sems.at[2 + part]))
+    for index in range(parts):
+        source = w_hbm.at[pl.ds(index * depth, depth), pl.ds(2 * width, width)]
+        copies.append(pltpu.make_async_copy(source, w_ref.at[index], in_sems.at[2 + index]))
     for copy in copies:
         copy.start()
 
@@ -76,19 +74,23 @@
     outs[0].start()
 
     copies[1].wait()
-    for index in range(steps):
-        pair = []
-        for offset, part in enumerate((index, steps + index)):
-            copies[2 + 2 * index + offset].wait()
-            query = silu(dot(cand_ref[...], w_ref[part])).astype(BF16)
-            pair.append(dot(place, query).reshape(slots // 8, 8, block))
-        even, odd = weave(*pair)
-        columns = pl.ds(index * block, block)
-        out_ref[:, 0, :, columns] = even.astype(BF16)
-        out_ref[:, 1, :, columns] = odd.astype(BF16)
-        copy = pltpu.make_async_copy(
-            out_ref.at[:, :, :, columns], out_hbm.at[:, :, :, columns], out_sems.at[1 + index]
-        )
+    total = None
+    for index in range(parts):
+        copies[2 + index].wait()
+        term = dot(cand_ref[:, index * depth : (index + 1) * depth], w_ref[index])
+        total = term if total is None else total + term
+    query = silu(total).astype(BF16)
+    half = width // 2
+    pieces = out_sems.shape[0] - 1
+    count = slots // pieces
+    tiles = count // 8
+    for index in range(pieces):
+        moved = dot(place[index * count : (index + 1) * count], query).reshape(tiles, 8, width)
+        even, odd = weave(moved[:, :, :half], moved[:, :, half:])
+        span = pl.ds(index * tiles, tiles)
+        out_ref[span, 0] = even.astype(BF16)
+        out_ref[span, 1] = odd.astype(BF16)
+        copy = pltpu.make_async_copy(out_ref.at[span], out_hbm.at[span], out_sems.at[1 + index])
         copy.start()
         outs.append(copy)
     for copy in outs:
@@ -99,8 +101,8 @@
     rows, width = candidates.shape
     half = width // 2
     slots = users * CAP
-    block = 256
-    parts = width // block
+    parts = 4
+    pieces = 4
     whole = pl.BlockSpec(memory_space=pl.ANY)
     tiles = (slots // 8, 2, 8, half)
     return pl.pallas_call(
@@ -114,11 +116,11 @@
         scratch_shapes=[
             pltpu.VMEM((1, rows), jnp.int32),
             pltpu.VMEM((rows, width), BF16),
-            pltpu.VMEM((parts, width, block), BF16),
+            pltpu.VMEM((parts, width // parts, width), BF16),
             pltpu.VMEM(tiles, BF16),
             pltpu.VMEM((slots, rows), BF16),
             pltpu.SemaphoreType.DMA((parts + 2,)),
-            pltpu.SemaphoreType.DMA((parts // 2 + 1,)),
+            pltpu.SemaphoreType.DMA((pieces + 1,)),
         ],
         compiler_params=params(),
         cost_estimate=pl.CostEstimate(
@@ -200,7 +202,6 @@
                 copy.start()
     scale = 0.5 / math.sqrt(head_size)
     got_copy.wait()
-    outs = []
     for pair in range(pairs):
         columns = pl.ds(pair * head_size, head_size)
         for head in (pair, pairs + pair):
@@ -216,13 +217,9 @@
         even, odd = weave(*results)
         out_ref[:, 0, :, columns] = even.astype(BF16)
         out_ref[:, 1, :, columns] = odd.astype(BF16)
-        copy = pltpu.make_async_copy(
-            out_ref.at[:, :, :, columns], out_hbm.at[:, :, :, columns], out_sems.at[pair]
-        )
-        copy.start()
-        outs.append(copy)
-    for copy in outs:
-        copy.wait()
+    copy = pltpu.make_async_copy(out_ref, out_hbm, out_sems.at[0])
+    copy.start()
+    copy.wait()
 
 
 def attention(got, keys, values):
@@ -340,14 +337,15 @@
     normed = (scaled * own_ref[:, 2 * width : 3 * width].astype(F32)).astype(BF16)
     w_copy.wait()
     cand_copy.wait()
-    block = 256
+    pieces = out_sems.shape[0]
+    count = cand_ref.shape[0] // pieces
     outs = []
-    for index in range(width // block):
-        columns = slice(index * block, (index + 1) * block)
-        result = cand_ref[:, columns].astype(F32) + dot(normed, w_ref[:, columns])
-        out_ref[:, columns] = result.astype(BF16)
-        span = pl.ds(index * block, block)
-        copy = pltpu.make_async_copy(out_ref.at[:, span], out_hbm.at[:, span], out_sems.at[index])
+    for index in range(pieces):
+        span = slice(index * count, (index + 1) * count)
+        result = cand_ref[span].astype(F32) + dot(normed[span], w_ref[...])
+        out_ref[span] = result.astype(BF16)
+        block = pl.ds(index * count, count)
+        copy = pltpu.make_async_copy(out_ref.at[block], out_hbm.at[block], out_sems.at[index])
         copy.start()
         outs.append(copy)
     for copy in outs:
@@ -366,7 +364,7 @@
         + [
             pltpu.VMEM((rows, width), BF16),
             pltpu.SemaphoreType.DMA((6,)),
-            pltpu.SemaphoreType.DMA((width // 256,)),
+            pltpu.SemaphoreType.DMA((2,)),
         ],
         compiler_params=params(51),
         cost_estimate=pl.CostEstimate(

time: 100 us -> 99 us (0.990)
  Pallas kernels: 37.8 us -> 36.7 us
    pallas_call x1, Pallas kernels: 4.82 us -> 3.52 us  [front(): pl.pallas_call(front_kernel, in_specs=[whole] * 3, out_specs=[whole] * 2,...]
where the time goes in v4:
time: 99 us; the launch traced here: 98.5 us
  waiting for transfers between devices  37.2 us (38%)
  Pallas kernels  36.7 us (37%)
  starting transfers between devices  22.1 us (22%)
  local copies, waits for them, and re-layouts  1.01 us (1%)
    all_to_all x2, waiting for transfers between devices, exchange(): lax.all_to_all(flat, 'serve', split_axis=0, concat_axis=0, tiled=True)  35.8 us
    all_to_all x2, starting transfers between devices, exchange(): lax.all_to_all(flat, 'serve', split_axis=0, concat_axis=0, tiled=True)  22 us
    pallas_call x1, Pallas kernels, keys_vals(): pl.pallas_call(functools.partial(keys_vals_kernel, steps), grid=(2 * step...  13.7 us
    pallas_call x1, Pallas kernels, attention(): pl.pallas_call(attention_kernel, in_specs=[whole] * 3, out_specs=whole, o...  7.92 us
    pallas_call x1, Pallas kernels, own_part(): pl.pallas_call(functools.partial(own_kernel, width // HEADS), grid=(steps...  7.86 us
    pallas_call x1, Pallas kernels, tail(): pl.pallas_call(tail_kernel, in_specs=[pl.BlockSpec(memory_space=pl.ANY)]...  3.74 us
    pallas_call x1, Pallas kernels, front(): pl.pallas_call(front_kernel, in_specs=[whole] * 3, out_specs=[whole] * 2,...  3.52 us
  transfers between devices with their start and end apart: 3, of which 3 were waited for; matrix products, arithmetic and copies ran while one was open for 1% of the time, Pallas kernels for 22%

profile of v4, /device:TPU:32, one launch (start us, length us, event | category | flops | bytes accessed | tf_op | source)
XLA Modules:
  0.0 98.5 jit_solution(17986726048821663859)
XLA Ops:
  0.0 3.5 %front.1 = (bf16[64,2,8,512]{3,2,1,0:T(8,128)(2,1)}, bf16[512,256]{1,0:T(8,128)(2,1)}) custom-call(s32[1,256]{1,0:T(1,128)} %bitcast.9, bf16[256,1024]{1,0:T(8,128)(2,1)} %cand_hbm.3, bf16[1024,4096]{1,0:T(8,128)(2,1)} %wk_ref.1), custom_call_target="tpu_custom_call" | custom-call | flops 805306368 | bytes 5242880 | tf_op jit(solution)/shard_map/front/pallas_call | solution.py:108
  3.5 0.0 copy-start.1
  3.5 15.1 %all-to-all-start = ((bf16[128,8,512]{2,1,0:T(8,128)(2,1)}), bf16[128,8,512]{2,1,0:T(8,128)(2,1)S(1)}, u32[]{:S(2)}, u32[]{:S(2)}) async-start(bf16[128,8,512]{2,1,0:T(8,128)(2,1)} %bitcast.8), calls=%async_computation | async-start | bytes 2097152 | tf_op jit(solution)/shard_map/all_to_all | solution.py:380
  18.7 0.0 copy-done.1
  18.7 0.1 collective-permute-start
  19.5 0.6 pad_add_fusion.info_ref
  20.1 1.4 %collective-permute-done.other_ref = bf16[512,1024]{1,0:T(8,128)(2,1)S(1)} collective-permute-done((bf16[512,1024]{1,0:T(8,128)(2,1)S(1)}, bf16[512,1024]{1,0:T(8,128)(2,1)S(1)}, u32[]{:S(2)}, u32[]{:S(2)}) %collective-permute-start) | collective-permute-done | bytes 1048608 | tf_op jit(solution)/shard_map/ppermute | solution.py:386
  21.5 0.0 copy-start.2
  21.5 1.0 %copy-done.2 = bf16[512,1024]{1,0:T(8,128)(2,1)} copy-done((bf16[512,1024]{1,0:T(8,128)(2,1)}, bf16[512,1024]{1,0:T(8,128)(2,1)S(1)}, u32[]{:S(2)}) %copy-start.2) | copy-done | bytes 1048600
  22.5 13.7 %keys_vals.1 = (bf16[1024,1024]{1,0:T(8,128)(2,1)}, bf16[8,1024,128]{2,1,0:T(8,128)(2,1)}) custom-call(s32[2]{0:T(128)} %pad_add_fusion.info_ref, bf16[512,1024]{1,0:T(8,128)(2,1)} %own_ref, bf16[512,1024]{1,0:T(8,128)(2,1)} %copy-done.2, bf16[1024,4096]{1,0:T(8,128)(2,1)} %wk_ref.1), custom_call_target="tpu_custom_call" | custom-call | flops 4294967296 | bytes 10485760 | tf_op jit(solution)/shard_map/keys_vals/pallas_call | solution.py:161
  36.1 13.9 %all-to-all-done = bf16[128,8,512]{2,1,0:T(8,128)(2,1)S(1)} async-done(((bf16[128,8,512]{2,1,0:T(8,128)(2,1)}), bf16[128,8,512]{2,1,0:T(8,128)(2,1)S(1)}, u32[]{:S(2)}, u32[]{:S(2)}) %all-to-all-start) | async-done | bytes 1048608 | tf_op jit(solution)/shard_map/all_to_all | solution.py:380
  50.1 7.9 %attention.1 = bf16[64,2,8,512]{3,2,1,0:T(8,128)(2,1)} custom-call(bf16[64,2,8,512]{3,2,1,0:T(8,128)(2,1)S(1)} %bitcast.7, bf16[1024,1024]{1,0:T(8,128)(2,1)} %get-tuple-element.16.key_hbm, bf16[8,1024,128]{2,1,0:T(8,128)(2,1)} %get-tuple-element.17.value_hbm), custom_call_target="tpu_custom_call" | custom-call | flops 2147483648 | bytes 6291456 | tf_op jit(solution)/shard_map/attention/pallas_call | solution.py:230
  58.0 6.8 %all-to-all-start.1 = ((bf16[128,8,512]{2,1,0:T(8,128)(2,1)}), bf16[128,8,512]{2,1,0:T(8,128)(2,1)S(1)}, u32[]{:S(2)}, u32[]{:S(2)}) async-start(bf16[128,8,512]{2,1,0:T(8,128)(2,1)} %bitcast.4), calls=%async_computation.1 | async-start | bytes 2097152 | tf_op jit(solution)/shard_map/all_to_all | solution.py:380
  64.8 0.0 copy-start
  64.8 7.9 %own_part.1.own_hbm = bf16[256,3584]{1,0:T(8,128)(2,1)} custom-call(bf16[256,1024]{1,0:T(8,128)(2,1)} %cand_hbm.3, bf16[1024,4096]{1,0:T(8,128)(2,1)} %wk_ref.1, bf16[1024,4096]{1,0:T(8,128)(2,1)} %wk_ref.1, bf16[1024,4096]{1,0:T(8,128)(2,1)} %wk_ref.1, bf16[1024,4096]{1,0:T(8,128)(2,1)} %wk_ref.1, bf16[512,256]{1,0:T(8,128)(2,1)} %get-tuple-element.18.place_ref), custom_call_target="tpu_custom_call" | custom-call | flops 2147483648 | bytes 11534336 | tf_op jit(solution)/shard_map/own_part/pallas_call | solution.py:287
  72.7 21.9 %all-to-all-done.1 = bf16[128,8,512]{2,1,0:T(8,128)(2,1)S(1)} async-done(((bf16[128,8,512]{2,1,0:T(8,128)(2,1)}), bf16[128,8,512]{2,1,0:T(8,128)(2,1)S(1)}, u32[]{:S(2)}, u32[]{:S(2)}) %all-to-all-start.1) | async-done | bytes 1048608 | tf_op jit(solution)/shard_map/all_to_all | solution.py:380
  94.6 0.0 copy-done
  94.6 3.7 %tail.1 = bf16[256,1024]{1,0:T(8,128)(2,1)} custom-call(bf16[64,2,8,512]{3,2,1,0:T(8,128)(2,1)S(1)} %bitcast.6, bf16[256,3584]{1,0:T(8,128)(2,1)} %own_part.1.own_hbm, bf16[256,1024]{1,0:T(8,128)(2,1)S(1)} %copy-done, bf16[1024,1024]{1,0:T(8,128)(2,1)} %w_hbm.3), custom_call_target="tpu_custom_call" | custom-call | flops 805306368 | bytes 6291456 | tf_op jit(solution)/shard_map/tail/pallas_call | solution.py:358
Async XLA Ops:
  3.5 15.2 %copy-start.1 = (bf16[512,1024]{1,0:T(8,128)(2,1)S(1)}, bf16[512,1024]{1,0:T(8,128)(2,1)}, u32[]{:S(2)}) copy-start(bf16[512,1024]{1,0:T(8,128)(2,1)} %own_ref) | copy-start | bytes 3145732
  3.5 46.5 %all-to-all-start = ((bf16[128,8,512]{2,1,0:T(8,128)(2,1)}), bf16[128,8,512]{2,1,0:T(8,128)(2,1)S(1)}, u32[]{:S(2)}, u32[]{:S(2)}) async-start(bf16[128,8,512]{2,1,0:T(8,128)(2,1)} %bitcast.8), calls=%async_computation | async-start | bytes 2097152 | tf_op jit(solution)/shard_map/all_to_all | solution.py:380
  18.7 2.7 %collective-permute-start = (bf16[512,1024]{1,0:T(8,128)(2,1)S(1)}, bf16[512,1024]{1,0:T(8,128)(2,1)S(1)}, u32[]{:S(2)}, u32[]{:S(2)}) collective-permute-start(bf16[512,1024]{1,0:T(8,128)(2,1)S(1)} %copy-done.1), channel_id=1, source_target_pairs={{0,1},{1,0},{2,3},{3,2},{4,5},{5,4},{6,7},{7,6},{8,9},{9,8},{10,11... | collective-permute-start | bytes 3145736 | tf_op jit(solution)/shard_map/ppermute | solution.py:386
  21.5 1.0 %copy-start.2 = (bf16[512,1024]{1,0:T(8,128)(2,1)}, bf16[512,1024]{1,0:T(8,128)(2,1)S(1)}, u32[]{:S(2)}) copy-start(bf16[512,1024]{1,0:T(8,128)(2,1)S(1)} %collective-permute-done.other_ref) | copy-start | bytes 3145732
  58.0 36.6 %all-to-all-start.1 = ((bf16[128,8,512]{2,1,0:T(8,128)(2,1)}), bf16[128,8,512]{2,1,0:T(8,128)(2,1)S(1)}, u32[]{:S(2)}, u32[]{:S(2)}) async-start(bf16[128,8,512]{2,1,0:T(8,128)(2,1)} %bitcast.4), calls=%async_computation.1 | async-start | bytes 2097152 | tf_op jit(solution)/shard_map/all_to_all | solution.py:380
  64.8 29.8 %copy-start = (bf16[256,1024]{1,0:T(8,128)(2,1)S(1)}, bf16[256,1024]{1,0:T(8,128)(2,1)}, u32[]{:S(2)}) copy-start(bf16[256,1024]{1,0:T(8,128)(2,1)} %cand_hbm.3) | copy-start | bytes 1572868

commit v5 on v4

--- a/solution.py
+++ b/solution.py
@@ -183,13 +183,11 @@
     )(info, own, other, w_uvqk)
 
 
-def attention_kernel(got_hbm, key_hbm, value_hbm, out_hbm, got_ref, key_ref, value_ref, out_ref, in_sems, out_sems):
+def attention_kernel(got_ref, key_hbm, value_hbm, out_hbm, key_ref, value_ref, out_ref, in_sems, out_sems):
     tiles, _, _, half = got_ref.shape
     slots = tiles * 8
     head_size = 2 * half // HEADS
     pairs = HEADS // 2
-    got_copy = pltpu.make_async_copy(got_hbm, got_ref, in_sems.at[2 * HEADS])
-    got_copy.start()
     copies = {}
     for pair in range(pairs):
         for head in (pair, pairs + pair):
@@ -201,25 +199,31 @@
             for copy in copies[head]:
                 copy.start()
     scale = 0.5 / math.sqrt(head_size)
-    got_copy.wait()
-    for pair in range(pairs):
-        columns = pl.ds(pair * head_size, head_size)
-        for head in (pair, pairs + pair):
-            for copy in copies[head]:
-                copy.wait()
-        queries = weave(got_ref[:, 0, :, columns].astype(F32), got_ref[:, 1, :, columns].astype(F32))
-        results = []
-        for query, head in zip(queries, (pair, pairs + pair)):
-            rows = query.reshape(slots, head_size).astype(BF16)
-            y = dot(rows, key_ref[head]) * scale
-            weights = (y + y * jnp.tanh(y)).astype(BF16)
-            results.append(dot(weights, value_ref[head]).reshape(tiles, 8, head_size))
-        even, odd = weave(*results)
-        out_ref[:, 0, :, columns] = even.astype(BF16)
-        out_ref[:, 1, :, columns] = odd.astype(BF16)
-    copy = pltpu.make_async_copy(out_ref, out_hbm, out_sems.at[0])
-    copy.start()
-    copy.wait()
+    outs = []
+    for group in ((0,), (1, 2, 3)):
+        for pair in group:
+            for head in (pair, pairs + pair):
+                for copy in copies[head]:
+                    copy.wait()
+        for pair in group:
+            columns = pl.ds(pair * head_size, head_size)
+            queries = weave(got_ref[:, 0, :, columns].astype(F32), got_ref[:, 1, :, columns].astype(F32))
+            results = []
+            for query, head in zip(queries, (pair, pairs + pair)):
+                rows = query.reshape(slots, head_size).astype(BF16)
+                y = dot(rows, key_ref[head]) * scale
+                weights = (y + y * jnp.tanh(y)).astype(BF16)
+                results.append(dot(weights, value_ref[head]).reshape(tiles, 8, head_size))
+            even, odd = weave(*results)
+            out_ref[:, 0, :, columns] = even.astype(BF16)
+            out_ref[:, 1, :, columns] = odd.astype(BF16)
+            copy = pltpu.make_async_copy(
+                out_ref.at[:, :, :, columns], out_hbm.at[:, :, :, columns], out_sems.at[pair]
+            )
+            copy.start()
+            outs.append(copy)
+    for copy in outs:
+        copy.wait()
 
 
 def attention(got, keys, values):
@@ -229,15 +233,14 @@
     whole = pl.BlockSpec(memory_space=pl.ANY)
     return pl.pallas_call(
         attention_kernel,
-        in_specs=[whole] * 3,
+        in_specs=[pl.BlockSpec(memory_space=pltpu.VMEM), whole, whole],
         out_specs=whole,
         out_shape=jax.ShapeDtypeStruct(got.shape, BF16),
         scratch_shapes=[
-            pltpu.VMEM(got.shape, BF16),
             pltpu.VMEM((heads, head_size, events), BF16),
             pltpu.VMEM((heads, events, head_size), BF16),
             pltpu.VMEM(got.shape, BF16),
-            pltpu.SemaphoreType.DMA((2 * heads + 1,)),
+            pltpu.SemaphoreType.DMA((2 * heads,)),
             pltpu.SemaphoreType.DMA((heads // 2,)),
         ],
         compiler_params=params(50),
@@ -297,7 +300,7 @@
         ],
         out_specs=pl.BlockSpec((rows, 3 * width + slots), lambda j: (0, 0)),
         out_shape=jax.ShapeDtypeStruct((rows, 3 * width + slots), BF16),
-        compiler_params=params(),
+        compiler_params=params(50),
         cost_estimate=pl.CostEstimate(
             flops=8 * rows * width * width, bytes_accessed=11 << 20, transcendentals=4 * rows * width
         ),
@@ -305,38 +308,23 @@
     )(candidates, w_uvqk, w_uvqk, w_uvqk, w_uvqk, place)
 
 
-def tail_kernel(
-    got_hbm, own_hbm, cand_hbm, w_hbm, out_hbm, got_ref, own_ref, cand_ref, w_ref, out_ref, in_sems, out_sems
-):
+def tail_kernel(got_ref, own_ref, cand_ref, w_hbm, out_hbm, w_ref, out_ref, in_sem, out_sems):
     tiles, _, _, half = got_ref.shape
     width = 2 * half
     slots = tiles * 8
-    spans = (pl.ds(3 * width, slots), pl.ds(0, 2 * width), pl.ds(2 * width, width))
-    got_copy = pltpu.make_async_copy(got_hbm, got_ref, in_sems.at[0])
-    place_copy, term_copy, gate_copy = (
-        pltpu.make_async_copy(own_hbm.at[:, span], own_ref.at[:, span], in_sems.at[1 + index])
-        for index, span in enumerate(spans)
-    )
-    w_copy = pltpu.make_async_copy(w_hbm, w_ref, in_sems.at[4])
-    cand_copy = pltpu.make_async_copy(cand_hbm, cand_ref, in_sems.at[5])
-    for copy in (got_copy, place_copy, term_copy, gate_copy, w_copy, cand_copy):
-        copy.start()
-    got_copy.wait()
-    place_copy.wait()
+    w_copy = pltpu.make_async_copy(w_hbm, w_ref, in_sem.at[0])
+    w_copy.start()
     place = own_ref[:, 3 * width : 3 * width + slots]
     parts = weave(got_ref[:, 0].astype(F32), got_ref[:, 1].astype(F32))
     history = [dot(place, part.reshape(slots, half).astype(BF16)) for part in parts]
-    term_copy.wait()
     term = own_ref[:, :width].astype(F32) + own_ref[:, width : 2 * width].astype(F32)
     attended = jnp.concatenate(history, 1) + term
     mean = jnp.sum(attended, 1, keepdims=True) / width
     centred = attended - mean
     var = jnp.sum(centred * centred, 1, keepdims=True) / width
     scaled = centred * lax.rsqrt(var + 1e-05)
-    gate_copy.wait()
     normed = (scaled * own_ref[:, 2 * width : 3 * width].astype(F32)).astype(BF16)
     w_copy.wait()
-    cand_copy.wait()
     pieces = out_sems.shape[0]
     count = cand_ref.shape[0] // pieces
     outs = []
@@ -354,24 +342,24 @@
 
 def tail(got, own, candidates, w_out):
     rows, width = candidates.shape
-    sources = (got, own, candidates, w_out)
+    inside = pl.BlockSpec(memory_space=pltpu.VMEM)
     return pl.pallas_call(
         tail_kernel,
-        in_specs=[pl.BlockSpec(memory_space=pl.ANY)] * 4,
+        in_specs=[inside] * 3 + [pl.BlockSpec(memory_space=pl.ANY)],
         out_specs=pl.BlockSpec(memory_space=pl.ANY),
         out_shape=jax.ShapeDtypeStruct((rows, width), BF16),
-        scratch_shapes=[pltpu.VMEM(source.shape, source.dtype) for source in sources]
-        + [
+        scratch_shapes=[
+            pltpu.VMEM(w_out.shape, BF16),
             pltpu.VMEM((rows, width), BF16),
-            pltpu.SemaphoreType.DMA((6,)),
+            pltpu.SemaphoreType.DMA((1,)),
             pltpu.SemaphoreType.DMA((2,)),
         ],
-        compiler_params=params(51),
+        compiler_params=params(50),
         cost_estimate=pl.CostEstimate(
             flops=2 * rows * width * (width + got.shape[0] * 8), bytes_accessed=6 << 20, transcendentals=rows
         ),
         name="tail",
-    )(*sources)
+    )(got, own, candidates, w_out)
 
 
 def exchange(rows):

time: 99 us -> 97.7 us (0.987)
  Pallas kernels: 36.7 us -> 33.6 us
    pallas_call x1, Pallas kernels: 7.86 us -> 6.17 us  [own_part(): pl.pallas_call(functools.partial(own_kernel, width // HEADS), grid=(steps...]
    pallas_call x2, Pallas kernels: 11.7 us -> 10.2 us  [the longest x1 7.14 us: attention(): pl.pallas_call(attention_kernel, in_specs=[pl.BlockSpec(memory_space=pltp...]
  transfers between devices with their start and end apart: 3 -> 3, of which waited for: 3 -> 3; matrix products, arithmetic and copies ran while one was open for 1% -> 1% of each run, Pallas kernels for 22% -> 20%
where the time goes in v5:
time: 97.7 us; the launch traced here: 97.2 us
  waiting for transfers between devices  37.9 us (39%)
  Pallas kernels  33.6 us (34%)
  starting transfers between devices  22.2 us (23%)
  local copies, waits for them, and re-layouts  1.96 us (2%)
    all_to_all x2, waiting for transfers between devices, exchange(): lax.all_to_all(flat, 'serve', split_axis=0, concat_axis=0, tiled=True)  36.5 us
    all_to_all x2, starting transfers between devices, exchange(): lax.all_to_all(flat, 'serve', split_axis=0, concat_axis=0, tiled=True)  22.1 us
    pallas_call x1, Pallas kernels, keys_vals(): pl.pallas_call(functools.partial(keys_vals_kernel, steps), grid=(2 * step...  13.7 us
    pallas_call x1, Pallas kernels, attention(): pl.pallas_call(attention_kernel, in_specs=[pl.BlockSpec(memory_space=pltp...  7.14 us
    pallas_call x1, Pallas kernels, own_part(): pl.pallas_call(functools.partial(own_kernel, width // HEADS), grid=(steps...  6.17 us
    pallas_call x1, Pallas kernels, front(): pl.pallas_call(front_kernel, in_specs=[whole] * 3, out_specs=[whole] * 2,...  3.52 us
    pallas_call x1, Pallas kernels, tail(): pl.pallas_call(tail_kernel, in_specs=[inside] * 3 + [pl.BlockSpec(memory_...  3.04 us
    unnamed x8, local copies, waits for them, and re-layouts  1.96 us
  transfers between devices with their start and end apart: 3, of which 3 were waited for; matrix products, arithmetic and copies ran while one was open for 1% of the time, Pallas kernels for 20%

profile of v5, /device:TPU:32, one launch (start us, length us, event | category | flops | bytes accessed | tf_op | source)
XLA Modules:
  0.0 97.2 jit_solution(6542084982289970325)
XLA Ops:
  0.0 3.5 %front.1 = (bf16[64,2,8,512]{3,2,1,0:T(8,128)(2,1)}, bf16[512,256]{1,0:T(8,128)(2,1)}) custom-call(s32[1,256]{1,0:T(1,128)} %bitcast.9, bf16[256,1024]{1,0:T(8,128)(2,1)} %cand_ref.3, bf16[1024,4096]{1,0:T(8,128)(2,1)} %wk_ref.1), custom_call_target="tpu_custom_call" | custom-call | flops 805306368 | bytes 5242880 | tf_op jit(solution)/shard_map/front/pallas_call | solution.py:108
  3.5 0.0 copy-start.2
  3.5 15.1 %all-to-all-start = ((bf16[128,8,512]{2,1,0:T(8,128)(2,1)}), bf16[128,8,512]{2,1,0:T(8,128)(2,1)S(1)}, u32[]{:S(2)}, u32[]{:S(2)}) async-start(bf16[128,8,512]{2,1,0:T(8,128)(2,1)} %bitcast.8), calls=%async_computation | async-start | bytes 2097152 | tf_op jit(solution)/shard_map/all_to_all | solution.py:368
  18.7 0.0 copy-done.2
  18.7 0.1 collective-permute-start
  19.5 0.6 pad_add_fusion.info_ref
  20.1 1.4 %collective-permute-done.other_ref = bf16[512,1024]{1,0:T(8,128)(2,1)S(1)} collective-permute-done((bf16[512,1024]{1,0:T(8,128)(2,1)S(1)}, bf16[512,1024]{1,0:T(8,128)(2,1)S(1)}, u32[]{:S(2)}, u32[]{:S(2)}) %collective-permute-start) | collective-permute-done | bytes 1048608 | tf_op jit(solution)/shard_map/ppermute | solution.py:374
  21.5 0.0 copy-start.3
  21.5 1.0 %copy-done.3 = bf16[512,1024]{1,0:T(8,128)(2,1)} copy-done((bf16[512,1024]{1,0:T(8,128)(2,1)}, bf16[512,1024]{1,0:T(8,128)(2,1)S(1)}, u32[]{:S(2)}) %copy-start.3) | copy-done | bytes 1048600
  22.5 13.7 %keys_vals.1 = (bf16[1024,1024]{1,0:T(8,128)(2,1)}, bf16[8,1024,128]{2,1,0:T(8,128)(2,1)}) custom-call(s32[2]{0:T(128)} %pad_add_fusion.info_ref, bf16[512,1024]{1,0:T(8,128)(2,1)} %own_ref, bf16[512,1024]{1,0:T(8,128)(2,1)} %copy-done.3, bf16[1024,4096]{1,0:T(8,128)(2,1)} %wk_ref.1), custom_call_target="tpu_custom_call" | custom-call | flops 4294967296 | bytes 10485760 | tf_op jit(solution)/shard_map/keys_vals/pallas_call | solution.py:161
  36.2 13.9 %all-to-all-done = bf16[128,8,512]{2,1,0:T(8,128)(2,1)S(1)} async-done(((bf16[128,8,512]{2,1,0:T(8,128)(2,1)}), bf16[128,8,512]{2,1,0:T(8,128)(2,1)S(1)}, u32[]{:S(2)}, u32[]{:S(2)}) %all-to-all-start) | async-done | bytes 1048608 | tf_op jit(solution)/shard_map/all_to_all | solution.py:368
  50.1 7.1 %attention.1 = bf16[64,2,8,512]{3,2,1,0:T(8,128)(2,1)} custom-call(bf16[64,2,8,512]{3,2,1,0:T(8,128)(2,1)S(1)} %bitcast.7, bf16[1024,1024]{1,0:T(8,128)(2,1)} %get-tuple-element.16.key_hbm, bf16[8,1024,128]{2,1,0:T(8,128)(2,1)} %get-tuple-element.17.value_hbm), custom_call_target="tpu_custom_call" | custom-call | flops 2147483648 | bytes 6291456 | tf_op jit(solution)/shard_map/attention/pallas_call | solution.py:234
  57.2 0.0 copy-start
  57.2 7.0 %all-to-all-start.1 = ((bf16[128,8,512]{2,1,0:T(8,128)(2,1)}), bf16[128,8,512]{2,1,0:T(8,128)(2,1)S(1)}, u32[]{:S(2)}, u32[]{:S(2)}) async-start(bf16[128,8,512]{2,1,0:T(8,128)(2,1)} %bitcast.4), calls=%async_computation.1 | async-start | bytes 2097152 | tf_op jit(solution)/shard_map/all_to_all | solution.py:368
  64.2 0.0 copy-done
  64.2 0.0 copy-start.1
  64.2 0.9 copy-done.1
  65.2 6.2 %own_part.1.own_ref = bf16[256,3584]{1,0:T(8,128)(2,1)S(1)} custom-call(bf16[256,1024]{1,0:T(8,128)(2,1)S(1)} %copy-done, bf16[1024,4096]{1,0:T(8,128)(2,1)} %wk_ref.1, bf16[1024,4096]{1,0:T(8,128)(2,1)} %wk_ref.1, bf16[1024,4096]{1,0:T(8,128)(2,1)} %wk_ref.1, bf16[1024,4096]{1,0:T(8,128)(2,1)} %wk_ref.1, bf16[512,256]{1,0:T(8,128)(2,1)S(1)} %copy-done.1), custom_call_target="tpu_custom_call" | custom-call | flops 2147483648 | bytes 11534336 | tf_op jit(solution)/shard_map/own_part/pallas_call | solution.py:290
  71.3 22.6 %all-to-all-done.1 = bf16[128,8,512]{2,1,0:T(8,128)(2,1)S(1)} async-done(((bf16[128,8,512]{2,1,0:T(8,128)(2,1)}), bf16[128,8,512]{2,1,0:T(8,128)(2,1)S(1)}, u32[]{:S(2)}, u32[]{:S(2)}) %all-to-all-start.1) | async-done | bytes 1048608 | tf_op jit(solution)/shard_map/all_to_all | solution.py:368
  94.0 3.0 %tail.1 = bf16[256,1024]{1,0:T(8,128)(2,1)} custom-call(bf16[64,2,8,512]{3,2,1,0:T(8,128)(2,1)S(1)} %bitcast.6, bf16[256,3584]{1,0:T(8,128)(2,1)S(1)} %own_part.1.own_ref, bf16[256,1024]{1,0:T(8,128)(2,1)S(1)} %copy-done, bf16[1024,1024]{1,0:T(8,128)(2,1)} %w_hbm.3), custom_call_target="tpu_custom_call" | custom-call | flops 805306368 | bytes 6291456 | tf_op jit(solution)/shard_map/tail/pallas_call | solution.py:346
Async XLA Ops:
  3.5 15.2 %copy-start.2 = (bf16[512,1024]{1,0:T(8,128)(2,1)S(1)}, bf16[512,1024]{1,0:T(8,128)(2,1)}, u32[]{:S(2)}) copy-start(bf16[512,1024]{1,0:T(8,128)(2,1)} %own_ref) | copy-start | bytes 3145732
  3.5 46.5 %all-to-all-start = ((bf16[128,8,512]{2,1,0:T(8,128)(2,1)}), bf16[128,8,512]{2,1,0:T(8,128)(2,1)S(1)}, u32[]{:S(2)}, u32[]{:S(2)}) async-start(bf16[128,8,512]{2,1,0:T(8,128)(2,1)} %bitcast.8), calls=%async_computation | async-start | bytes 2097152 | tf_op jit(solution)/shard_map/all_to_all | solution.py:368
  18.7 2.7 %collective-permute-start = (bf16[512,1024]{1,0:T(8,128)(2,1)S(1)}, bf16[512,1024]{1,0:T(8,128)(2,1)S(1)}, u32[]{:S(2)}, u32[]{:S(2)}) collective-permute-start(bf16[512,1024]{1,0:T(8,128)(2,1)S(1)} %copy-done.2), channel_id=1, source_target_pairs={{0,1},{1,0},{2,3},{3,2},{4,5},{5,4},{6,7},{7,6},{8,9},{9,8},{10,11... | collective-permute-start | bytes 3145736 | tf_op jit(solution)/shard_map/ppermute | solution.py:374
  21.5 1.0 %copy-start.3 = (bf16[512,1024]{1,0:T(8,128)(2,1)}, bf16[512,1024]{1,0:T(8,128)(2,1)S(1)}, u32[]{:S(2)}) copy-start(bf16[512,1024]{1,0:T(8,128)(2,1)S(1)} %collective-permute-done.other_ref) | copy-start | bytes 3145732
  57.2 7.0 %copy-start = (bf16[256,1024]{1,0:T(8,128)(2,1)S(1)}, bf16[256,1024]{1,0:T(8,128)(2,1)}, u32[]{:S(2)}) copy-start(bf16[256,1024]{1,0:T(8,128)(2,1)} %cand_ref.3) | copy-start | bytes 1572868
  57.2 36.8 %all-to-all-start.1 = ((bf16[128,8,512]{2,1,0:T(8,128)(2,1)}), bf16[128,8,512]{2,1,0:T(8,128)(2,1)S(1)}, u32[]{:S(2)}, u32[]{:S(2)}) async-start(bf16[128,8,512]{2,1,0:T(8,128)(2,1)} %bitcast.4), calls=%async_computation.1 | async-start | bytes 2097152 | tf_op jit(solution)/shard_map/all_to_all | solution.py:368
  64.2 1.0 copy-start.1

commit v6 on v5

--- a/solution.py
+++ b/solution.py
@@ -130,31 +130,27 @@
     )(cand_user.reshape(1, rows), candidates, w_uvqk)
 
 
-def keys_vals_kernel(steps, info_ref, own_ref, other_ref, w_ref, key_ref, value_ref):
+def keys_vals_kernel(steps, info_ref, own_ref, w_ref, key_ref, value_ref):
     count = own_ref.shape[0]
-    weight = w_ref[...]
-    for part, ref in enumerate((own_ref, other_ref)):
-        result = silu(dot(ref[...], weight))
-        span = slice(part * count, (part + 1) * count)
-
-        @pl.when(pl.program_id(0) < steps)
-        def _():
-            row = lax.broadcasted_iota(jnp.int32, (count, count), 0)
-            column = lax.broadcasted_iota(jnp.int32, (count, count), 1)
-            identity = jnp.where(row == column, 1.0, 0.0).astype(BF16)
-            key_ref[:, span] = turn(result.astype(BF16), identity)
-
-        @pl.when(pl.program_id(0) >= steps)
-        def _():
-            start = jnp.where(info_ref[1] == part, 0, count)
-            event = start + lax.broadcasted_iota(jnp.int32, result.shape, 0)
-            value = jnp.where(event < info_ref[0], result, 0.0).astype(BF16)
-            head_size = value_ref.shape[2]
-            for head in range(value_ref.shape[0]):
-                value_ref[head, span] = value[:, head * head_size : (head + 1) * head_size]
-
-
-def keys_vals(info, own, other, w_uvqk):
+    result = silu(dot(own_ref[...], w_ref[...]))
+
+    @pl.when(pl.program_id(0) < steps)
+    def _():
+        row = lax.broadcasted_iota(jnp.int32, (count, count), 0)
+        column = lax.broadcasted_iota(jnp.int32, (count, count), 1)
+        identity = jnp.where(row == column, 1.0, 0.0).astype(BF16)
+        key_ref[...] = turn(result.astype(BF16), identity)
+
+    @pl.when(pl.program_id(0) >= steps)
+    def _():
+        event = info_ref[1] * count + lax.broadcasted_iota(jnp.int32, result.shape, 0)
+        value = jnp.where(event < info_ref[0], result, 0.0).astype(BF16)
+        head_size = value_ref.shape[2]
+        for head in range(value_ref.shape[0]):
+            value_ref[head] = value[:, head * head_size : (head + 1) * head_size]
+
+
+def keys_vals(info, own, w_uvqk):
     count, width = own.shape
     block = min(256, width)
     steps = width // block
@@ -164,38 +160,46 @@
         in_specs=[
             pl.BlockSpec(memory_space=pltpu.SMEM),
             pl.BlockSpec((count, width), lambda j: (0, 0)),
-            pl.BlockSpec((count, width), lambda j: (0, 0)),
             pl.BlockSpec((width, block), lambda j: (0, jnp.where(j < steps, 3 * steps + j, j))),
         ],
         out_specs=[
-            pl.BlockSpec((block, 2 * count), lambda j: (jnp.minimum(j, steps - 1), 0)),
-            pl.BlockSpec((HEADS // steps, 2 * count, width // HEADS), lambda j: (jnp.maximum(j - steps, 0), 0, 0)),
+            pl.BlockSpec((block, count), lambda j: (jnp.minimum(j, steps - 1), 0)),
+            pl.BlockSpec((HEADS // steps, count, width // HEADS), lambda j: (jnp.maximum(j - steps, 0), 0, 0)),
         ],
         out_shape=[
-            jax.ShapeDtypeStruct((width, 2 * count), BF16),
-            jax.ShapeDtypeStruct((HEADS, 2 * count, width // HEADS), BF16),
+            jax.ShapeDtypeStruct((width, count), BF16),
+            jax.ShapeDtypeStruct((HEADS, count, width // HEADS), BF16),
         ],
         compiler_params=params(),
         cost_estimate=pl.CostEstimate(
-            flops=8 * count * width * width, bytes_accessed=10 << 20, transcendentals=4 * count * width
+            flops=4 * count * width * width, bytes_accessed=7 << 20, transcendentals=2 * count * width
         ),
         name="keys_vals",
-    )(info, own, other, w_uvqk)
-
-
-def attention_kernel(got_ref, key_hbm, value_hbm, out_hbm, key_ref, value_ref, out_ref, in_sems, out_sems):
+    )(info, own, w_uvqk)
+
+
+def attention_kernel(
+    got_ref, key0_hbm, key1_hbm, value0_hbm, value1_hbm, out_hbm, key_ref, value_ref, out_ref, in_sems, out_sems):
     tiles, _, _, half = got_ref.shape
     slots = tiles * 8
     head_size = 2 * half // HEADS
     pairs = HEADS // 2
+    key_hbms, value_hbms = (key0_hbm, key1_hbm), (value0_hbm, value1_hbm)
     copies = {}
+    count = key_hbms[0].shape[1]
     for pair in range(pairs):
         for head in (pair, pairs + pair):
             rows = pl.ds(head * head_size, head_size)
-            copies[head] = (
-                pltpu.make_async_copy(key_hbm.at[rows], key_ref.at[head], in_sems.at[head]),
-                pltpu.make_async_copy(value_hbm.at[head], value_ref.at[head], in_sems.at[HEADS + head]),
-            )
+            copies[head] = []
+            for part in range(2):
+                span = pl.ds(part * count, count)
+                sem = in_sems.at[head, part]
+                copies[head].append(
+                    pltpu.make_async_copy(key_hbms[part].at[rows], key_ref.at[head, :, span], sem.at[0])
+                )
+                copies[head].append(
+                    pltpu.make_async_copy(value_hbms[part].at[head], value_ref.at[head, span], sem.at[1])
+                )
             for copy in copies[head]:
                 copy.start()
     scale = 0.5 / math.sqrt(head_size)
@@ -229,28 +233,29 @@
 def attention(got, keys, values):
     tiles, _, _, half = got.shape
     slots = tiles * 8
-    heads, events, head_size = values.shape
+    heads, count, head_size = values[0].shape
+    events = 2 * count
     whole = pl.BlockSpec(memory_space=pl.ANY)
     return pl.pallas_call(
         attention_kernel,
-        in_specs=[pl.BlockSpec(memory_space=pltpu.VMEM), whole, whole],
+        in_specs=[pl.BlockSpec(memory_space=pltpu.VMEM)] + [whole] * 4,
         out_specs=whole,
         out_shape=jax.ShapeDtypeStruct(got.shape, BF16),
         scratch_shapes=[
             pltpu.VMEM((heads, head_size, events), BF16),
             pltpu.VMEM((heads, events, head_size), BF16),
             pltpu.VMEM(got.shape, BF16),
-            pltpu.SemaphoreType.DMA((2 * heads,)),
+            pltpu.SemaphoreType.DMA((heads, 2, 2)),
             pltpu.SemaphoreType.DMA((heads // 2,)),
         ],
-        compiler_params=params(50),
+        compiler_params=params(51),
         cost_estimate=pl.CostEstimate(
             flops=8 * slots * events * half,
             bytes_accessed=6 << 20,
             transcendentals=slots * events * heads,
         ),
         name="attention",
-    )(got, keys, values)
+    )(got, *keys, *values)
 
 
 def own_kernel(head_size, cand_ref, wg_ref, wv_ref, wq_ref, wk_ref, place_ref, out_ref):
@@ -371,13 +376,15 @@
 def per_device(history, candidates, cand_user, hist_len, w_uvqk, w_out):
     users = lax.axis_size("serve")
     outgoing, place = front(cand_user, candidates, w_uvqk, users)
-    other = lax.ppermute(history, "rep", [(0, 1), (1, 0)])
     outgoing, history, place = lax.optimization_barrier((outgoing, history, place))
     received = exchange(outgoing)
     info = jnp.concatenate([hist_len, lax.axis_index("rep").astype(jnp.int32)[None]])
-    keys, values = keys_vals(info, history, other, w_uvqk)
+    key, value = keys_vals(info, history, w_uvqk)
+    key, value, place = lax.optimization_barrier((key, value, place))
+    other_key, other_value = (lax.ppermute(half, "rep", [(0, 1), (1, 0)]) for half in (key, value))
     own = own_part(candidates, w_uvqk, place)
-    returned = exchange(attention(received, keys, values))
+    received, own = lax.optimization_barrier((received, own))
+    returned = exchange(attention(received, (key, other_key), (value, other_value)))
     return tail(returned, own, candidates, w_out)
 
 

time: 97.7 us -> 97 us (level)
  blocking collectives: 0 us -> 36 us
  waiting for transfers between devices: 37.9 us -> 14.1 us
  starting transfers between devices: 22.2 us -> 15.5 us
  Pallas kernels: 33.6 us -> 29.5 us
  local copies, waits for them, and re-layouts: 1.96 us -> 0.01 us
    all_to_all x0 -> x1, blocking collectives: none -> 36 us  [exchange(): lax.all_to_all(flat, 'serve', split_axis=0, concat_axis=0, tiled=True)]
    all_to_all x2 -> x1, waiting for transfers between devices: 36.5 us -> 14.1 us  [exchange(): lax.all_to_all(flat, 'serve', split_axis=0, concat_axis=0, tiled=True)]
    all_to_all x2 -> x1, starting transfers between devices: 22.1 us -> 15 us  [exchange(): lax.all_to_all(flat, 'serve', split_axis=0, concat_axis=0, tiled=True)]
    pallas_call x1, Pallas kernels: 13.7 us -> 9.28 us  [keys_vals(): pl.pallas_call(functools.partial(keys_vals_kernel, steps), grid=(2 * step...]
    unnamed x8 -> x4, local copies, waits for them, and re-layouts: 1.96 us -> 0.01 us
    ppermute x1 -> x2, waiting for transfers between devices: 1.4 us -> 0.01 us  [per_device(): lax.ppermute(half, 'rep', [(0, 1), (1, 0)])]
  transfers between devices with their start and end apart: 3 -> 3, of which waited for: 3 -> 1; matrix products, arithmetic and copies ran while one was open for 1% -> 1% of each run, Pallas kernels for 20% -> 16%
where the time goes in v6:
time: 97 us; the launch traced here: 96.5 us
  blocking collectives  36 us (37%)
  Pallas kernels  29.5 us (30%)
  starting transfers between devices  15.5 us (16%)
  waiting for transfers between devices  14.1 us (15%)
    all_to_all x1, blocking collectives, exchange(): lax.all_to_all(flat, 'serve', split_axis=0, concat_axis=0, tiled=True)  36 us
    all_to_all x1, starting transfers between devices, exchange(): lax.all_to_all(flat, 'serve', split_axis=0, concat_axis=0, tiled=True)  15 us
    all_to_all x1, waiting for transfers between devices, exchange(): lax.all_to_all(flat, 'serve', split_axis=0, concat_axis=0, tiled=True)  14.1 us
    pallas_call x1, Pallas kernels, keys_vals(): pl.pallas_call(functools.partial(keys_vals_kernel, steps), grid=(2 * step...  9.28 us
    pallas_call x1, Pallas kernels, attention(): pl.pallas_call(attention_kernel, in_specs=[pl.BlockSpec(memory_space=pltp...  7.42 us
    pallas_call x1, Pallas kernels, own_part(): pl.pallas_call(functools.partial(own_kernel, width // HEADS), grid=(steps...  6.18 us
    pallas_call x1, Pallas kernels, front(): pl.pallas_call(front_kernel, in_specs=[whole] * 3, out_specs=[whole] * 2,...  3.53 us
    pallas_call x1, Pallas kernels, tail(): pl.pallas_call(tail_kernel, in_specs=[inside] * 3 + [pl.BlockSpec(memory_...  3.04 us
  transfers between devices with their start and end apart: 3, of which 1 were waited for; matrix products, arithmetic and copies ran while one was open for 1% of the time, Pallas kernels for 16%

profile of v6, /device:TPU:32, one launch (start us, length us, event | category | flops | bytes accessed | tf_op | source)
XLA Modules:
  0.0 96.5 jit_solution(11029307399456517594)
XLA Ops:
  0.0 3.5 %front.1 = (bf16[64,2,8,512]{3,2,1,0:T(8,128)(2,1)}, bf16[512,256]{1,0:T(8,128)(2,1)}) custom-call(s32[1,256]{1,0:T(1,128)} %bitcast.10, bf16[256,1024]{1,0:T(8,128)(2,1)} %cand_ref.3, bf16[1024,4096]{1,0:T(8,128)(2,1)} %wk_ref.1), custom_call_target="tpu_custom_call" | custom-call | flops 805306368 | bytes 5242880 | tf_op jit(solution)/shard_map/front/pallas_call | solution.py:108
  3.5 15.0 %all-to-all-start = ((bf16[128,8,512]{2,1,0:T(8,128)(2,1)}), bf16[128,8,512]{2,1,0:T(8,128)(2,1)S(1)}, u32[]{:S(2)}, u32[]{:S(2)}) async-start(bf16[128,8,512]{2,1,0:T(8,128)(2,1)} %bitcast.9), calls=%async_computation | async-start | bytes 2097152 | tf_op jit(solution)/shard_map/all_to_all | solution.py:373
  19.2 0.6 pad_add_fusion.info_ref
  19.8 0.0 copy-start
  19.8 0.0 copy-start.1
  19.8 9.3 %keys_vals.1 = (bf16[1024,512]{1,0:T(8,128)(2,1)}, bf16[8,512,128]{2,1,0:T(8,128)(2,1)}) custom-call(s32[2]{0:T(128)} %pad_add_fusion.info_ref, bf16[512,1024]{1,0:T(8,128)(2,1)} %own_ref, bf16[1024,4096]{1,0:T(8,128)(2,1)} %wk_ref.1), custom_call_target="tpu_custom_call" | custom-call | flops 2147483648 | bytes 7340032 | tf_op jit(solution)/shard_map/keys_vals/pallas_call | solution.py:157
  29.1 0.0 collective-permute-start
  29.1 0.5 collective-permute-start.1
  29.6 0.0 copy-done
  29.6 0.0 copy-done.1
  29.6 6.2 %own_part.1.own_ref = bf16[256,3584]{1,0:T(8,128)(2,1)S(1)} custom-call(bf16[256,1024]{1,0:T(8,128)(2,1)S(1)} %copy-done, bf16[1024,4096]{1,0:T(8,128)(2,1)} %wk_ref.1, bf16[1024,4096]{1,0:T(8,128)(2,1)} %wk_ref.1, bf16[1024,4096]{1,0:T(8,128)(2,1)} %wk_ref.1, bf16[1024,4096]{1,0:T(8,128)(2,1)} %wk_ref.1, bf16[512,256]{1,0:T(8,128)(2,1)S(1)} %copy-done.1), custom_call_target="tpu_custom_call" | custom-call | flops 2147483648 | bytes 11534336 | tf_op jit(solution)/shard_map/own_part/pallas_call | solution.py:295
  35.8 14.1 %all-to-all-done = bf16[128,8,512]{2,1,0:T(8,128)(2,1)S(1)} async-done(((bf16[128,8,512]{2,1,0:T(8,128)(2,1)}), bf16[128,8,512]{2,1,0:T(8,128)(2,1)S(1)}, u32[]{:S(2)}, u32[]{:S(2)}) %all-to-all-start) | async-done | bytes 1048608 | tf_op jit(solution)/shard_map/all_to_all | solution.py:373
  49.9 0.0 collective-permute-done.key1_hbm
  49.9 0.0 collective-permute-done.1.value1_hbm
  49.9 7.4 %attention.1 = bf16[64,2,8,512]{3,2,1,0:T(8,128)(2,1)S(1)} custom-call(bf16[64,2,8,512]{3,2,1,0:T(8,128)(2,1)S(1)} %bitcast.7, bf16[1024,512]{1,0:T(8,128)(2,1)} %get-tuple-element.26.key0_hbm, bf16[1024,512]{1,0:T(8,128)(2,1)} %collective-permute-done.key1_hbm, bf16[8,512,128]{2,1,0:T(8,128)(2,1)} %get-tuple-element.27.value0_hbm, ...), custom_call_target="tpu_custom_call" | custom-call | flops 2147483648 | bytes 6291456 | tf_op jit(solution)/shard_map/attention/pallas_call | solution.py:239
  57.4 36.0 %all_to_all.10 = bf16[128,8,512]{2,1,0:T(8,128)(2,1)S(1)} all-to-all(bf16[128,8,512]{2,1,0:T(8,128)(2,1)S(1)} %bitcast.8), channel_id=1, replica_groups=mesh['serve'=128,'rep'=2] {'serve'}, dimensions={0} | all-to-all | bytes 2097152 | tf_op jit(solution)/shard_map/all_to_all | solution.py:373
  93.3 3.0 %tail.1 = bf16[256,1024]{1,0:T(8,128)(2,1)} custom-call(bf16[64,2,8,512]{3,2,1,0:T(8,128)(2,1)S(1)} %bitcast.6, bf16[256,3584]{1,0:T(8,128)(2,1)S(1)} %own_part.1.own_ref, bf16[256,1024]{1,0:T(8,128)(2,1)S(1)} %copy-done, bf16[1024,1024]{1,0:T(8,128)(2,1)} %w_hbm.3), custom_call_target="tpu_custom_call" | custom-call | flops 805306368 | bytes 6291456 | tf_op jit(solution)/shard_map/tail/pallas_call | solution.py:351
Async XLA Ops:
  3.5 46.4 %all-to-all-start = ((bf16[128,8,512]{2,1,0:T(8,128)(2,1)}), bf16[128,8,512]{2,1,0:T(8,128)(2,1)S(1)}, u32[]{:S(2)}, u32[]{:S(2)}) async-start(bf16[128,8,512]{2,1,0:T(8,128)(2,1)} %bitcast.9), calls=%async_computation | async-start | bytes 2097152 | tf_op jit(solution)/shard_map/all_to_all | solution.py:373
  19.8 9.8 %copy-start = (bf16[256,1024]{1,0:T(8,128)(2,1)S(1)}, bf16[256,1024]{1,0:T(8,128)(2,1)}, u32[]{:S(2)}) copy-start(bf16[256,1024]{1,0:T(8,128)(2,1)} %cand_ref.3) | copy-start | bytes 1572868
  19.8 9.8 %copy-start.1 = (bf16[512,256]{1,0:T(8,128)(2,1)S(1)}, bf16[512,256]{1,0:T(8,128)(2,1)}, u32[]{:S(2)}) copy-start(bf16[512,256]{1,0:T(8,128)(2,1)} %get-tuple-element.24.place_ref) | copy-start | bytes 786436
  29.1 20.8 %collective-permute-start = (bf16[1024,512]{1,0:T(8,128)(2,1)}, bf16[1024,512]{1,0:T(8,128)(2,1)}, u32[]{:S(2)}, u32[]{:S(2)}) collective-permute-start(bf16[1024,512]{1,0:T(8,128)(2,1)} %get-tuple-element.26.key0_hbm), channel_id=1, source_target_pairs={{0,1},{1,0},{2,3},{3,2},{4,5},{5,4},{6,7},{7,6},{8,9},{9,8},{10,11... | collective-permute-start | bytes 3145736 | tf_op jit(solution)/shard_map/ppermute | solution.py:384
  29.1 20.8 %collective-permute-start.1 = (bf16[8,512,128]{2,1,0:T(8,128)(2,1)}, bf16[8,512,128]{2,1,0:T(8,128)(2,1)}, u32[]{:S(2)}, u32[]{:S(2)}) collective-permute-start(bf16[8,512,128]{2,1,0:T(8,128)(2,1)} %get-tuple-element.27.value0_hbm), channel_id=1, source_target_pairs={{0,1},{1,0},{2,3},{3,2},{4,5},{5,4},{6,7},{7,6},{8,9},{9,8},{10,11... | collective-permute-start | bytes 3145736 | tf_op jit(solution)/shard_map/ppermute | solution.py:384

commit v7 on v6

--- a/solution.py
+++ b/solution.py
@@ -179,7 +179,8 @@
 
 
 def attention_kernel(
-    got_ref, key0_hbm, key1_hbm, value0_hbm, value1_hbm, out_hbm, key_ref, value_ref, out_ref, in_sems, out_sems):
+    got_ref, key0_hbm, key1_hbm, value0_hbm, value1_hbm, out_ref, key_ref, value_ref, in_sems
+):
     tiles, _, _, half = got_ref.shape
     slots = tiles * 8
     head_size = 2 * half // HEADS
@@ -203,7 +204,6 @@
             for copy in copies[head]:
                 copy.start()
     scale = 0.5 / math.sqrt(head_size)
-    outs = []
     for group in ((0,), (1, 2, 3)):
         for pair in group:
             for head in (pair, pairs + pair):
@@ -221,13 +221,6 @@
             even, odd = weave(*results)
             out_ref[:, 0, :, columns] = even.astype(BF16)
             out_ref[:, 1, :, columns] = odd.astype(BF16)
-            copy = pltpu.make_async_copy(
-                out_ref.at[:, :, :, columns], out_hbm.at[:, :, :, columns], out_sems.at[pair]
-            )
-            copy.start()
-            outs.append(copy)
-    for copy in outs:
-        copy.wait()
 
 
 def attention(got, keys, values):
@@ -239,14 +232,12 @@
     return pl.pallas_call(
         attention_kernel,
         in_specs=[pl.BlockSpec(memory_space=pltpu.VMEM)] + [whole] * 4,
-        out_specs=whole,
+        out_specs=pl.BlockSpec(memory_space=pltpu.VMEM),
         out_shape=jax.ShapeDtypeStruct(got.shape, BF16),
         scratch_shapes=[
             pltpu.VMEM((heads, head_size, events), BF16),
             pltpu.VMEM((heads, events, head_size), BF16),
-            pltpu.VMEM(got.shape, BF16),
             pltpu.SemaphoreType.DMA((heads, 2, 2)),
-            pltpu.SemaphoreType.DMA((heads // 2,)),
         ],
         compiler_params=params(51),
         cost_estimate=pl.CostEstimate(

time: 97 us -> 96.2 us (level)
  no operation moved by 1% of the time
where the time goes in v7:
time: 96.2 us; the launch traced here: 95.8 us
  blocking collectives  36 us (37%)
  Pallas kernels  28.7 us (30%)
  starting transfers between devices  15.5 us (16%)
  waiting for transfers between devices  14.1 us (15%)
    all_to_all x1, blocking collectives, exchange(): lax.all_to_all(flat, 'serve', split_axis=0, concat_axis=0, tiled=True)  36 us
    all_to_all x1, starting transfers between devices, exchange(): lax.all_to_all(flat, 'serve', split_axis=0, concat_axis=0, tiled=True)  15 us
    all_to_all x1, waiting for transfers between devices, exchange(): lax.all_to_all(flat, 'serve', split_axis=0, concat_axis=0, tiled=True)  14.1 us
    pallas_call x1, Pallas kernels, keys_vals(): pl.pallas_call(functools.partial(keys_vals_kernel, steps), grid=(2 * step...  9.28 us
    pallas_call x1, Pallas kernels, attention(): pl.pallas_call(attention_kernel, in_specs=[pl.BlockSpec(memory_space=pltp...  6.64 us
    pallas_call x1, Pallas kernels, own_part(): pl.pallas_call(functools.partial(own_kernel, width // HEADS), grid=(steps...  6.18 us
    pallas_call x1, Pallas kernels, front(): pl.pallas_call(front_kernel, in_specs=[whole] * 3, out_specs=[whole] * 2,...  3.53 us
    pallas_call x1, Pallas kernels, tail(): pl.pallas_call(tail_kernel, in_specs=[inside] * 3 + [pl.BlockSpec(memory_...  3.04 us
  transfers between devices with their start and end apart: 3, of which 1 were waited for; matrix products, arithmetic and copies ran while one was open for 1% of the time, Pallas kernels for 16%

profile of v7, /device:TPU:32, one launch (start us, length us, event | category | flops | bytes accessed | tf_op | source)
XLA Modules:
  0.0 95.8 jit_solution(7938141313162653317)
XLA Ops:
  0.0 3.5 %front.1 = (bf16[64,2,8,512]{3,2,1,0:T(8,128)(2,1)}, bf16[512,256]{1,0:T(8,128)(2,1)}) custom-call(s32[1,256]{1,0:T(1,128)} %bitcast.10, bf16[256,1024]{1,0:T(8,128)(2,1)} %cand_ref.3, bf16[1024,4096]{1,0:T(8,128)(2,1)} %wk_ref.1), custom_call_target="tpu_custom_call" | custom-call | flops 805306368 | bytes 5242880 | tf_op jit(solution)/shard_map/front/pallas_call | solution.py:108
  3.5 15.0 %all-to-all-start = ((bf16[128,8,512]{2,1,0:T(8,128)(2,1)}), bf16[128,8,512]{2,1,0:T(8,128)(2,1)S(1)}, u32[]{:S(2)}, u32[]{:S(2)}) async-start(bf16[128,8,512]{2,1,0:T(8,128)(2,1)} %bitcast.9), calls=%async_computation | async-start | bytes 2097152 | tf_op jit(solution)/shard_map/all_to_all | solution.py:364
  19.2 0.6 pad_add_fusion.info_ref
  19.8 0.0 copy-start
  19.8 0.0 copy-start.1
  19.8 9.3 %keys_vals.1 = (bf16[1024,512]{1,0:T(8,128)(2,1)}, bf16[8,512,128]{2,1,0:T(8,128)(2,1)}) custom-call(s32[2]{0:T(128)} %pad_add_fusion.info_ref, bf16[512,1024]{1,0:T(8,128)(2,1)} %own_ref, bf16[1024,4096]{1,0:T(8,128)(2,1)} %wk_ref.1), custom_call_target="tpu_custom_call" | custom-call | flops 2147483648 | bytes 7340032 | tf_op jit(solution)/shard_map/keys_vals/pallas_call | solution.py:157
  29.1 0.0 collective-permute-start
  29.1 0.5 collective-permute-start.1
  29.6 0.0 copy-done
  29.6 0.0 copy-done.1
  29.6 6.2 %own_part.1.own_ref = bf16[256,3584]{1,0:T(8,128)(2,1)S(1)} custom-call(bf16[256,1024]{1,0:T(8,128)(2,1)S(1)} %copy-done, bf16[1024,4096]{1,0:T(8,128)(2,1)} %wk_ref.1, bf16[1024,4096]{1,0:T(8,128)(2,1)} %wk_ref.1, bf16[1024,4096]{1,0:T(8,128)(2,1)} %wk_ref.1, bf16[1024,4096]{1,0:T(8,128)(2,1)} %wk_ref.1, bf16[512,256]{1,0:T(8,128)(2,1)S(1)} %copy-done.1), custom_call_target="tpu_custom_call" | custom-call | flops 2147483648 | bytes 11534336 | tf_op jit(solution)/shard_map/own_part/pallas_call | solution.py:286
  35.8 14.1 %all-to-all-done = bf16[128,8,512]{2,1,0:T(8,128)(2,1)S(1)} async-done(((bf16[128,8,512]{2,1,0:T(8,128)(2,1)}), bf16[128,8,512]{2,1,0:T(8,128)(2,1)S(1)}, u32[]{:S(2)}, u32[]{:S(2)}) %all-to-all-start) | async-done | bytes 1048608 | tf_op jit(solution)/shard_map/all_to_all | solution.py:364
  49.9 0.0 collective-permute-done.key1_hbm
  49.9 0.0 collective-permute-done.1.value1_hbm
  49.9 6.6 %attention.1 = bf16[64,2,8,512]{3,2,1,0:T(8,128)(2,1)S(1)} custom-call(bf16[64,2,8,512]{3,2,1,0:T(8,128)(2,1)S(1)} %bitcast.7, bf16[1024,512]{1,0:T(8,128)(2,1)} %get-tuple-element.26.key0_hbm, bf16[1024,512]{1,0:T(8,128)(2,1)} %collective-permute-done.key1_hbm, bf16[8,512,128]{2,1,0:T(8,128)(2,1)} %get-tuple-element.27.value0_hbm, ...), custom_call_target="tpu_custom_call" | custom-call | flops 2147483648 | bytes 6291456 | tf_op jit(solution)/shard_map/attention/pallas_call | solution.py:232
  56.6 36.0 %all_to_all.10 = bf16[128,8,512]{2,1,0:T(8,128)(2,1)S(1)} all-to-all(bf16[128,8,512]{2,1,0:T(8,128)(2,1)S(1)} %bitcast.8), channel_id=1, replica_groups=mesh['serve'=128,'rep'=2] {'serve'}, dimensions={0} | all-to-all | bytes 2097152 | tf_op jit(solution)/shard_map/all_to_all | solution.py:364
  92.6 3.0 %tail.1 = bf16[256,1024]{1,0:T(8,128)(2,1)} custom-call(bf16[64,2,8,512]{3,2,1,0:T(8,128)(2,1)S(1)} %bitcast.6, bf16[256,3584]{1,0:T(8,128)(2,1)S(1)} %own_part.1.own_ref, bf16[256,1024]{1,0:T(8,128)(2,1)S(1)} %copy-done, bf16[1024,1024]{1,0:T(8,128)(2,1)} %w_hbm.3), custom_call_target="tpu_custom_call" | custom-call | flops 805306368 | bytes 6291456 | tf_op jit(solution)/shard_map/tail/pallas_call | solution.py:342
Async XLA Ops:
  3.5 46.4 %all-to-all-start = ((bf16[128,8,512]{2,1,0:T(8,128)(2,1)}), bf16[128,8,512]{2,1,0:T(8,128)(2,1)S(1)}, u32[]{:S(2)}, u32[]{:S(2)}) async-start(bf16[128,8,512]{2,1,0:T(8,128)(2,1)} %bitcast.9), calls=%async_computation | async-start | bytes 2097152 | tf_op jit(solution)/shard_map/all_to_all | solution.py:364
  19.8 9.8 %copy-start = (bf16[256,1024]{1,0:T(8,128)(2,1)S(1)}, bf16[256,1024]{1,0:T(8,128)(2,1)}, u32[]{:S(2)}) copy-start(bf16[256,1024]{1,0:T(8,128)(2,1)} %cand_ref.3) | copy-start | bytes 1572868
  19.8 9.8 %copy-start.1 = (bf16[512,256]{1,0:T(8,128)(2,1)S(1)}, bf16[512,256]{1,0:T(8,128)(2,1)}, u32[]{:S(2)}) copy-start(bf16[512,256]{1,0:T(8,128)(2,1)} %get-tuple-element.24.place_ref) | copy-start | bytes 786436
  29.1 20.8 %collective-permute-start = (bf16[1024,512]{1,0:T(8,128)(2,1)}, bf16[1024,512]{1,0:T(8,128)(2,1)}, u32[]{:S(2)}, u32[]{:S(2)}) collective-permute-start(bf16[1024,512]{1,0:T(8,128)(2,1)} %get-tuple-element.26.key0_hbm), channel_id=1, source_target_pairs={{0,1},{1,0},{2,3},{3,2},{4,5},{5,4},{6,7},{7,6},{8,9},{9,8},{10,11... | collective-permute-start | bytes 3145736 | tf_op jit(solution)/shard_map/ppermute | solution.py:375
  29.1 20.8 %collective-permute-start.1 = (bf16[8,512,128]{2,1,0:T(8,128)(2,1)}, bf16[8,512,128]{2,1,0:T(8,128)(2,1)}, u32[]{:S(2)}, u32[]{:S(2)}) collective-permute-start(bf16[8,512,128]{2,1,0:T(8,128)(2,1)} %get-tuple-element.27.value0_hbm), channel_id=1, source_target_pairs={{0,1},{1,0},{2,3},{3,2},{4,5},{5,4},{6,7},{7,6},{8,9},{9,8},{10,11... | collective-permute-start | bytes 3145736 | tf_op jit(solution)/shard_map/ppermute | solution.py:375

commit v8 on v7

--- a/solution.py
+++ b/solution.py
@@ -304,12 +304,10 @@
     )(candidates, w_uvqk, w_uvqk, w_uvqk, w_uvqk, place)
 
 
-def tail_kernel(got_ref, own_ref, cand_ref, w_hbm, out_hbm, w_ref, out_ref, in_sem, out_sems):
+def tail_kernel(got_ref, own_ref, cand_ref, w_ref, out_hbm, out_ref, out_sems):
     tiles, _, _, half = got_ref.shape
     width = 2 * half
     slots = tiles * 8
-    w_copy = pltpu.make_async_copy(w_hbm, w_ref, in_sem.at[0])
-    w_copy.start()
     place = own_ref[:, 3 * width : 3 * width + slots]
     parts = weave(got_ref[:, 0].astype(F32), got_ref[:, 1].astype(F32))
     history = [dot(place, part.reshape(slots, half).astype(BF16)) for part in parts]
@@ -320,7 +318,6 @@
     var = jnp.sum(centred * centred, 1, keepdims=True) / width
     scaled = centred * lax.rsqrt(var + 1e-05)
     normed = (scaled * own_ref[:, 2 * width : 3 * width].astype(F32)).astype(BF16)
-    w_copy.wait()
     pieces = out_sems.shape[0]
     count = cand_ref.shape[0] // pieces
     outs = []
@@ -341,16 +338,14 @@
     inside = pl.BlockSpec(memory_space=pltpu.VMEM)
     return pl.pallas_call(
         tail_kernel,
-        in_specs=[inside] * 3 + [pl.BlockSpec(memory_space=pl.ANY)],
+        in_specs=[inside] * 4,
         out_specs=pl.BlockSpec(memory_space=pl.ANY),
         out_shape=jax.ShapeDtypeStruct((rows, width), BF16),
         scratch_shapes=[
-            pltpu.VMEM(w_out.shape, BF16),
             pltpu.VMEM((rows, width), BF16),
-            pltpu.SemaphoreType.DMA((1,)),
             pltpu.SemaphoreType.DMA((2,)),
         ],
-        compiler_params=params(50),
+        compiler_params=params(47),
         cost_estimate=pl.CostEstimate(
             flops=2 * rows * width * (width + got.shape[0] * 8), bytes_accessed=6 << 20, transcendentals=rows
         ),

time: 96.2 us -> 95.5 us (level)
  no operation moved by 1% of the time
where the time goes in v8:
time: 95.5 us; the launch traced here: 95 us
  blocking collectives  36.1 us (38%)
  Pallas kernels  27.8 us (29%)
  starting transfers between devices  15.5 us (16%)
  waiting for transfers between devices  14.1 us (15%)
    all_to_all x1, blocking collectives, exchange(): lax.all_to_all(flat, 'serve', split_axis=0, concat_axis=0, tiled=True)  36.1 us
    all_to_all x1, starting transfers between devices, exchange(): lax.all_to_all(flat, 'serve', split_axis=0, concat_axis=0, tiled=True)  15 us
    all_to_all x1, waiting for transfers between devices, exchange(): lax.all_to_all(flat, 'serve', split_axis=0, concat_axis=0, tiled=True)  14.1 us
    pallas_call x1, Pallas kernels, keys_vals(): pl.pallas_call(functools.partial(keys_vals_kernel, steps), grid=(2 * step...  9.29 us
    pallas_call x1, Pallas kernels, attention(): pl.pallas_call(attention_kernel, in_specs=[pl.BlockSpec(memory_space=pltp...  6.64 us
    pallas_call x1, Pallas kernels, own_part(): pl.pallas_call(functools.partial(own_kernel, width // HEADS), grid=(steps...  6.18 us
    pallas_call x1, Pallas kernels, front(): pl.pallas_call(front_kernel, in_specs=[whole] * 3, out_specs=[whole] * 2,...  3.53 us
    pallas_call x1, Pallas kernels, tail(): pl.pallas_call(tail_kernel, in_specs=[inside] * 4, out_specs=pl.BlockSpec...  2.18 us
  transfers between devices with their start and end apart: 3, of which 1 were waited for; matrix products, arithmetic and copies ran while one was open for 1% of the time, Pallas kernels for 16%

profile of v8, /device:TPU:32, one launch (start us, length us, event | category | flops | bytes accessed | tf_op | source)
XLA Modules:
  0.0 95.0 jit_solution(3903243106361969005)
XLA Ops:
  0.0 3.5 %front.1 = (bf16[64,2,8,512]{3,2,1,0:T(8,128)(2,1)}, bf16[512,256]{1,0:T(8,128)(2,1)}) custom-call(s32[1,256]{1,0:T(1,128)} %bitcast.10, bf16[256,1024]{1,0:T(8,128)(2,1)} %cand_ref.3, bf16[1024,4096]{1,0:T(8,128)(2,1)} %wk_ref.1), custom_call_target="tpu_custom_call" | custom-call | flops 805306368 | bytes 5242880 | tf_op jit(solution)/shard_map/front/pallas_call | solution.py:108
  3.5 15.0 %all-to-all-start = ((bf16[128,8,512]{2,1,0:T(8,128)(2,1)}), bf16[128,8,512]{2,1,0:T(8,128)(2,1)S(1)}, u32[]{:S(2)}, u32[]{:S(2)}) async-start(bf16[128,8,512]{2,1,0:T(8,128)(2,1)} %bitcast.9), calls=%async_computation | async-start | bytes 2097152 | tf_op jit(solution)/shard_map/all_to_all | solution.py:359
  19.2 0.6 pad_add_fusion.info_ref
  19.8 0.0 copy-start
  19.8 0.0 copy-start.2
  19.8 9.3 %keys_vals.1 = (bf16[1024,512]{1,0:T(8,128)(2,1)}, bf16[8,512,128]{2,1,0:T(8,128)(2,1)}) custom-call(s32[2]{0:T(128)} %pad_add_fusion.info_ref, bf16[512,1024]{1,0:T(8,128)(2,1)} %own_ref, bf16[1024,4096]{1,0:T(8,128)(2,1)} %wk_ref.1), custom_call_target="tpu_custom_call" | custom-call | flops 2147483648 | bytes 7340032 | tf_op jit(solution)/shard_map/keys_vals/pallas_call | solution.py:157
  29.1 0.0 collective-permute-start
  29.1 0.5 collective-permute-start.1
  29.6 0.0 copy-done
  29.6 0.0 copy-done.2
  29.6 6.2 %own_part.1.own_ref = bf16[256,3584]{1,0:T(8,128)(2,1)S(1)} custom-call(bf16[256,1024]{1,0:T(8,128)(2,1)S(1)} %copy-done, bf16[1024,4096]{1,0:T(8,128)(2,1)} %wk_ref.1, bf16[1024,4096]{1,0:T(8,128)(2,1)} %wk_ref.1, bf16[1024,4096]{1,0:T(8,128)(2,1)} %wk_ref.1, bf16[1024,4096]{1,0:T(8,128)(2,1)} %wk_ref.1, bf16[512,256]{1,0:T(8,128)(2,1)S(1)} %copy-done.2), custom_call_target="tpu_custom_call" | custom-call | flops 2147483648 | bytes 11534336 | tf_op jit(solution)/shard_map/own_part/pallas_call | solution.py:286
  35.8 14.1 %all-to-all-done = bf16[128,8,512]{2,1,0:T(8,128)(2,1)S(1)} async-done(((bf16[128,8,512]{2,1,0:T(8,128)(2,1)}), bf16[128,8,512]{2,1,0:T(8,128)(2,1)S(1)}, u32[]{:S(2)}, u32[]{:S(2)}) %all-to-all-start) | async-done | bytes 1048608 | tf_op jit(solution)/shard_map/all_to_all | solution.py:359
  49.9 0.0 collective-permute-done.key1_hbm
  49.9 0.0 collective-permute-done.1.value1_hbm
  49.9 6.6 %attention.1 = bf16[64,2,8,512]{3,2,1,0:T(8,128)(2,1)S(1)} custom-call(bf16[64,2,8,512]{3,2,1,0:T(8,128)(2,1)S(1)} %bitcast.7, bf16[1024,512]{1,0:T(8,128)(2,1)} %get-tuple-element.26.key0_hbm, bf16[1024,512]{1,0:T(8,128)(2,1)} %collective-permute-done.key1_hbm, bf16[8,512,128]{2,1,0:T(8,128)(2,1)} %get-tuple-element.27.value0_hbm, ...), custom_call_target="tpu_custom_call" | custom-call | flops 2147483648 | bytes 6291456 | tf_op jit(solution)/shard_map/attention/pallas_call | solution.py:232
  56.6 0.0 copy-start.1
  56.6 36.1 %all_to_all.10 = bf16[128,8,512]{2,1,0:T(8,128)(2,1)S(1)} all-to-all(bf16[128,8,512]{2,1,0:T(8,128)(2,1)S(1)} %bitcast.8), channel_id=1, replica_groups=mesh['serve'=128,'rep'=2] {'serve'}, dimensions={0} | all-to-all | bytes 2097152 | tf_op jit(solution)/shard_map/all_to_all | solution.py:359
  92.7 0.0 copy-done.1
  92.7 2.2 %tail.1 = bf16[256,1024]{1,0:T(8,128)(2,1)} custom-call(bf16[64,2,8,512]{3,2,1,0:T(8,128)(2,1)S(1)} %bitcast.6, bf16[256,3584]{1,0:T(8,128)(2,1)S(1)} %own_part.1.own_ref, bf16[256,1024]{1,0:T(8,128)(2,1)S(1)} %copy-done, bf16[1024,1024]{1,0:T(8,128)(2,1)S(1)} %copy-done.1), custom_call_target="tpu_custom_call" | custom-call | flops 805306368 | bytes 6291456 | tf_op jit(solution)/shard_map/tail/pallas_call | solution.py:339
Async XLA Ops:
  3.5 46.4 %all-to-all-start = ((bf16[128,8,512]{2,1,0:T(8,128)(2,1)}), bf16[128,8,512]{2,1,0:T(8,128)(2,1)S(1)}, u32[]{:S(2)}, u32[]{:S(2)}) async-start(bf16[128,8,512]{2,1,0:T(8,128)(2,1)} %bitcast.9), calls=%async_computation | async-start | bytes 2097152 | tf_op jit(solution)/shard_map/all_to_all | solution.py:359
  19.8 9.8 %copy-start = (bf16[256,1024]{1,0:T(8,128)(2,1)S(1)}, bf16[256,1024]{1,0:T(8,128)(2,1)}, u32[]{:S(2)}) copy-start(bf16[256,1024]{1,0:T(8,128)(2,1)} %cand_ref.3) | copy-start | bytes 1572868
  19.8 9.8 %copy-start.2 = (bf16[512,256]{1,0:T(8,128)(2,1)S(1)}, bf16[512,256]{1,0:T(8,128)(2,1)}, u32[]{:S(2)}) copy-start(bf16[512,256]{1,0:T(8,128)(2,1)} %get-tuple-element.24.place_ref) | copy-start | bytes 786436
  29.1 20.8 %collective-permute-start = (bf16[1024,512]{1,0:T(8,128)(2,1)}, bf16[1024,512]{1,0:T(8,128)(2,1)}, u32[]{:S(2)}, u32[]{:S(2)}) collective-permute-start(bf16[1024,512]{1,0:T(8,128)(2,1)} %get-tuple-element.26.key0_hbm), channel_id=1, source_target_pairs={{0,1},{1,0},{2,3},{3,2},{4,5},{5,4},{6,7},{7,6},{8,9},{9,8},{10,11... | collective-permute-start | bytes 3145736 | tf_op jit(solution)/shard_map/ppermute | solution.py:370
  29.1 20.8 %collective-permute-start.1 = (bf16[8,512,128]{2,1,0:T(8,128)(2,1)}, bf16[8,512,128]{2,1,0:T(8,128)(2,1)}, u32[]{:S(2)}, u32[]{:S(2)}) collective-permute-start(bf16[8,512,128]{2,1,0:T(8,128)(2,1)} %get-tuple-element.27.value0_hbm), channel_id=1, source_target_pairs={{0,1},{1,0},{2,3},{3,2},{4,5},{5,4},{6,7},{7,6},{8,9},{9,8},{10,11... | collective-permute-start | bytes 3145736 | tf_op jit(solution)/shard_map/ppermute | solution.py:370
  56.6 36.1 %copy-start.1 = (bf16[1024,1024]{1,0:T(8,128)(2,1)S(1)}, bf16[1024,1024]{1,0:T(8,128)(2,1)}, u32[]{:S(2)}) copy-start(bf16[1024,1024]{1,0:T(8,128)(2,1)} %w_ref.3) | copy-start | bytes 6291460
